TPU v7x, 128 devices: a whole 4x4x4 slice. The times are simulated.
128 devices in a mesh: space: 32 (over y, z, core), param: 4 (over x).
Axes of the slice: x: 4, y: 4, z: 4, core: 2. Of those that a mesh axis runs over, the one named last changes fastest.
Arguments:
- snapshots: float32 [196608, 4096], P('space', 'param'), may hold values from -1800 to 1800
- sketch: float32 [4096, 32], P('param'), may hold values from -0.09375 to 0.09375
- sketch_next: float32 [256, 32], replicated, may hold values from -0.375 to 0.375
Outputs:
- first_core: float32 [32, 196608], P(None, 'space')
- second_core: float32 [32, 512], P(None, 'param')
- remainder: float32 [32, 256], replicated
All inputs are finite; a program needn't handle non-finite values.
Results may differ from a plain program's by a relative error of at most 0.00016.
Values sent between devices are 32-bit elements; how exact they have to be, the bound alone decides.
A program may use at most 128 MiB of HBM per device.

v0:
```python
import math

import jax
import jax.numpy as jnp
from jax import lax
from jax.sharding import PartitionSpec as P

R = 32
N2 = 16
N3 = 16
ITERS = 3


def gram_matrix(block):
    return jnp.dot(block, block.T, precision=lax.Precision.HIGHEST)


def apply_factor(lower, block):
    return jax.scipy.linalg.solve_triangular(lower, block, lower=True)


def frame_space(block):
    lower = jnp.linalg.cholesky(lax.psum(gram_matrix(block), "space"))
    return apply_factor(lower, block)


def frame_param(block):
    lower = jnp.linalg.cholesky(lax.psum(gram_matrix(block), "param"))
    return apply_factor(lower, block)


def shards(snapshots, sketch, sketch_next):
    highest = lax.Precision.HIGHEST
    rows_total = snapshots.shape[0] * lax.axis_size("space")

    def new_basis(partial_value):
        return frame_space(lax.psum(partial_value, "param"))

    def project(basis):
        return lax.psum(jnp.dot(basis, snapshots, precision=highest), "space")

    partial_value = lax.dot_general(sketch, snapshots, (((0,), (1,)), ((), ())), precision=highest)
    basis = new_basis(partial_value)
    for step in range(ITERS):
        column_frame = frame_param(project(basis))
        partial_value = lax.dot_general(
            column_frame, snapshots, (((1,), (1,)), ((), ())), precision=highest
        )
        basis = new_basis(partial_value)
    coefficients = project(basis) / math.sqrt(rows_total)
    local_modes = coefficients.shape[1] // (N2 * N3)
    unfold = (
        coefficients.reshape(R, local_modes, N2 * N3)
        .transpose(1, 0, 2)
        .reshape(local_modes * R, N2 * N3)
    )
    second_sketch = lax.dot_general(
        sketch_next, unfold, (((0,), (1,)), ((), ())), precision=highest
    )
    second_frame = frame_param(second_sketch)
    next_rows = unfold.shape[0] * lax.axis_size("param")
    summed = lax.psum(jnp.dot(second_frame, unfold, precision=highest), "param")
    return (
        basis * math.sqrt(rows_total),
        second_frame * math.sqrt(next_rows),
        summed / math.sqrt(next_rows),
    )


def solution(mesh):
    placed = (P("space", "param"), P("param", None), P())
    return jax.shard_map(
        shards,
        mesh=mesh,
        in_specs=placed,
        out_specs=(P(None, "space"), P(None, "param"), P()),
        check_vma=False,
    )
```

profile of v0, /device:TPU:1, one launch (start us, length us, event | category | flops | bytes accessed | tf_op | source)
XLA Modules:
  0.0 1411.1 jit_solution(7739105379200843760)
XLA Ops:
  7.2 0.8 copy-done
  8.1 26.3 %fusion.44 = f32[32,6144]{1,0:T(8,128)} fusion(f32[1024,32]{0,1:T(8,128)S(1)} %copy-done, f32[6144,1024]{1,0:T(8,128)} %param.8), kind=kOutput, calls=%fused_computation.77 | convolution fusion | flops 2415919104 | bytes 26083328 | tf_op jit(solution)/shard_map/dot_general | solution.py:42
  34.5 45.9 %all-reduce.9.cloned.1.call-done = f32[32,6144]{1,0:T(8,128)} async-done(((f32[32,6144]{1,0:T(8,128)}), f32[32,6144]{1,0:T(8,128)}) %all-reduce.9.cloned.1.call-update) | async-done | bytes 786448 | tf_op jit(solution)/shard_map/psum | solution.py:37
  80.4 2.1 fusion.45
  82.5 123.3 %psum.120 = f32[32,32]{0,1:T(8,128)S(1)} all-reduce(f32[32,32]{0,1:T(8,128)S(1)} %fusion.45), channel_id=1, replica_groups=mesh['space'=32,'param'=4] {'space'}, use_global_device_ids=true, to_apply=%region_1.0 | all-reduce | flops 1024 | bytes 8192 | tf_op jit(solution)/shard_map/psum | solution.py:23
  205.9 2.9 cholesky.134
  209.5 0.7 fusion
  210.2 2.4 custom-call.18
  212.6 2.0 fusion.29
  214.6 18.2 %fusion.46 = f32[32,1024]{1,0:T(8,128)} fusion(f32[32,6144]{1,0:T(8,128)S(1)} %fusion.29, f32[6144,1024]{1,0:T(8,128)} %param.8), kind=kOutput, calls=%fused_computation.79 | convolution fusion | flops 2415919104 | bytes 26083328 | tf_op jit(solution)/shard_map/dot_general | solution.py:40
  232.8 100.3 %all-reduce.11.cloned.1.call-done = f32[32,1024]{1,0:T(8,128)} async-done(((f32[32,1024]{1,0:T(8,128)}), f32[32,1024]{1,0:T(8,128)}) %all-reduce.11.cloned.1.call-update) | async-done | bytes 131088 | tf_op jit(solution)/shard_map/psum | solution.py:40
  333.2 1.2 fusion.47
  334.4 13.6 psum.122
  348.1 2.9 cholesky.145
  351.7 0.7 fusion.1
  352.4 2.4 custom-call.19
  354.8 1.2 fusion.26
  356.0 26.3 %fusion.48 = f32[32,6144]{1,0:T(8,128)} fusion(f32[32,1024]{1,0:T(8,128)S(1)} %fusion.26, f32[6144,1024]{1,0:T(8,128)} %param.8), kind=kOutput, calls=%fused_computation.81 | convolution fusion | flops 2415919104 | bytes 26083328 | tf_op jit(solution)/shard_map/dot_general | solution.py:46
  382.4 43.5 %all-reduce.13.cloned.1.call-done = f32[32,6144]{1,0:T(8,128)} async-done(((f32[32,6144]{1,0:T(8,128)}), f32[32,6144]{1,0:T(8,128)}) %all-reduce.13.cloned.1.call-update) | async-done | bytes 786448 | tf_op jit(solution)/shard_map/psum | solution.py:37
  425.9 2.1 fusion.49
  428.0 123.3 %psum.124 = f32[32,32]{0,1:T(8,128)S(1)} all-reduce(f32[32,32]{0,1:T(8,128)S(1)} %fusion.49), channel_id=1, replica_groups=mesh['space'=32,'param'=4] {'space'}, use_global_device_ids=true, to_apply=%region_7.0 | all-reduce | flops 1024 | bytes 8192 | tf_op jit(solution)/shard_map/psum | solution.py:23
  551.4 2.9 cholesky.156
  555.0 0.7 fusion.2
  555.7 2.4 custom-call.20
  558.1 2.0 fusion.23
  560.1 18.1 %fusion.50 = f32[32,1024]{1,0:T(8,128)} fusion(f32[32,6144]{1,0:T(8,128)S(1)} %fusion.23, f32[6144,1024]{1,0:T(8,128)} %param.8), kind=kOutput, calls=%fused_computation.83 | convolution fusion | flops 2415919104 | bytes 26083328 | tf_op jit(solution)/shard_map/dot_general | solution.py:40
  578.3 100.3 %all-reduce.15.cloned.1.call-done = f32[32,1024]{1,0:T(8,128)} async-done(((f32[32,1024]{1,0:T(8,128)}), f32[32,1024]{1,0:T(8,128)}) %all-reduce.15.cloned.1.call-update) | async-done | bytes 131088 | tf_op jit(solution)/shard_map/psum | solution.py:40
  678.6 1.2 fusion.51
  679.9 13.3 psum.126
  693.3 2.9 cholesky.167
  696.9 0.7 fusion.3
  697.5 2.4 custom-call.21
  700.0 1.2 fusion.20
  701.2 26.3 %fusion.52 = f32[32,6144]{1,0:T(8,128)} fusion(f32[32,1024]{1,0:T(8,128)S(1)} %fusion.20, f32[6144,1024]{1,0:T(8,128)} %param.8), kind=kOutput, calls=%fused_computation.85 | convolution fusion | flops 2415919104 | bytes 26083328 | tf_op jit(solution)/shard_map/dot_general | solution.py:46
  727.6 43.5 %all-reduce.17.cloned.1.call-done = f32[32,6144]{1,0:T(8,128)} async-done(((f32[32,6144]{1,0:T(8,128)}), f32[32,6144]{1,0:T(8,128)}) %all-reduce.17.cloned.1.call-update) | async-done | bytes 786448 | tf_op jit(solution)/shard_map/psum | solution.py:37
  771.1 2.1 fusion.53
  773.3 123.3 %psum.128 = f32[32,32]{0,1:T(8,128)S(1)} all-reduce(f32[32,32]{0,1:T(8,128)S(1)} %fusion.53), channel_id=1, replica_groups=mesh['space'=32,'param'=4] {'space'}, use_global_device_ids=true, to_apply=%region_11.0 | all-reduce | flops 1024 | bytes 8192 | tf_op jit(solution)/shard_map/psum | solution.py:23
  896.7 2.9 cholesky.178
  900.3 0.7 fusion.4
  900.9 2.4 custom-call.22
  903.4 2.0 fusion.17
  905.4 18.2 %fusion.54 = f32[32,1024]{1,0:T(8,128)} fusion(f32[32,6144]{1,0:T(8,128)S(1)} %fusion.17, f32[6144,1024]{1,0:T(8,128)} %param.8), kind=kOutput, calls=%fused_computation.87 | convolution fusion | flops 2415919104 | bytes 26083328 | tf_op jit(solution)/shard_map/dot_general | solution.py:40
  923.6 100.3 %all-reduce.19.cloned.1.call-done = f32[32,1024]{1,0:T(8,128)} async-done(((f32[32,1024]{1,0:T(8,128)}), f32[32,1024]{1,0:T(8,128)}) %all-reduce.19.cloned.1.call-update) | async-done | bytes 131088 | tf_op jit(solution)/shard_map/psum | solution.py:40
  1023.9 1.2 fusion.55
  1025.1 13.4 psum.130
  1038.6 2.9 cholesky.189
  1042.2 0.7 fusion.5
  1042.8 2.4 custom-call.23
  1045.2 1.2 fusion.14
  1046.5 26.3 %fusion.56 = f32[32,6144]{1,0:T(8,128)} fusion(f32[32,1024]{1,0:T(8,128)S(1)} %fusion.14, f32[6144,1024]{1,0:T(8,128)} %param.8), kind=kOutput, calls=%fused_computation.89 | convolution fusion | flops 2415919104 | bytes 26083328 | tf_op jit(solution)/shard_map/dot_general | solution.py:46
  1072.9 43.5 %all-reduce.21.cloned.1.call-done = f32[32,6144]{1,0:T(8,128)} async-done(((f32[32,6144]{1,0:T(8,128)}), f32[32,6144]{1,0:T(8,128)}) %all-reduce.21.cloned.1.call-update) | async-done | bytes 786448 | tf_op jit(solution)/shard_map/psum | solution.py:37
  1116.4 2.1 fusion.57
  1118.5 123.3 %psum.132 = f32[32,32]{0,1:T(8,128)S(1)} all-reduce(f32[32,32]{0,1:T(8,128)S(1)} %fusion.57), channel_id=1, replica_groups=mesh['space'=32,'param'=4] {'space'}, use_global_device_ids=true, to_apply=%region_15.0 | all-reduce | flops 1024 | bytes 8192 | tf_op jit(solution)/shard_map/psum | solution.py:23
  1241.9 2.9 cholesky.200
  1246.2 2.4 custom-call.24
  1248.6 2.9 broadcast_multiply_fusion
  1251.5 18.1 %fusion.58 = f32[32,1024]{1,0:T(8,128)} fusion(f32[32,6144]{1,0:T(8,128)S(1)} %get-tuple-element.7, f32[6144,1024]{1,0:T(8,128)} %param.8), kind=kOutput, calls=%fused_computation.91 | convolution fusion | flops 2415919104 | bytes 26083328 | tf_op jit(solution)/shard_map/dot_general | solution.py:40
  1269.6 100.3 %all-reduce.23.cloned.1.call-done = f32[32,1024]{1,0:T(8,128)} async-done(((f32[32,1024]{1,0:T(8,128)}), f32[32,1024]{1,0:T(8,128)}) %all-reduce.23.cloned.1.call-update) | async-done | bytes 131088 | tf_op jit(solution)/shard_map/psum | solution.py:40
  1370.0 0.9 broadcast_multiply_fusion.1
  1371.3 13.1 psum.134
  1384.5 2.9 cholesky.211
  1388.7 2.4 custom-call.12
  1391.1 0.8 broadcast_multiply_fusion.3
  1392.2 11.2 psum.135
  (58 shorter events, 9.0 us)
Async XLA Ops:
  7.2 0.9 copy-start
  7.2 73.2 %all-reduce.9.cloned.1.call-start = ((), (), s32[]{:S(2)}) async-start(), calls=%async_computation | async-start | bytes 1572864 | tf_op jit(solution)/shard_map/psum | solution.py:37
  34.4 298.7 %all-reduce.11.cloned.1.call-start = ((), (), s32[]{:S(2)}) async-start(), calls=%async_computation.1 | async-start | bytes 262144 | tf_op jit(solution)/shard_map/psum | solution.py:40
  232.8 193.1 %all-reduce.13.cloned.1.call-start = ((), (), s32[]{:S(2)}) async-start(), calls=%async_computation.2 | async-start | bytes 1572864 | tf_op jit(solution)/shard_map/psum | solution.py:37
  382.4 296.2 %all-reduce.15.cloned.1.call-start = ((), (), s32[]{:S(2)}) async-start(), calls=%async_computation.3 | async-start | bytes 262144 | tf_op jit(solution)/shard_map/psum | solution.py:40
  578.3 192.9 %all-reduce.17.cloned.1.call-start = ((), (), s32[]{:S(2)}) async-start(), calls=%async_computation.4 | async-start | bytes 1572864 | tf_op jit(solution)/shard_map/psum | solution.py:37
  727.6 296.3 %all-reduce.19.cloned.1.call-start = ((), (), s32[]{:S(2)}) async-start(), calls=%async_computation.5 | async-start | bytes 262144 | tf_op jit(solution)/shard_map/psum | solution.py:40
  923.5 192.8 %all-reduce.21.cloned.1.call-start = ((), (), s32[]{:S(2)}) async-start(), calls=%async_computation.6 | async-start | bytes 1572864 | tf_op jit(solution)/shard_map/psum | solution.py:37
  1046.5 324.4 %copy-start.1 = (f32[256,32]{0,1:T(8,128)S(1)}, f32[256,32]{0,1:T(8,128)}, u32[]{:S(2)}) copy-start(f32[256,32]{0,1:T(8,128)} %param.10) | copy-start | bytes 98308
  1072.9 297.1 %all-reduce.23.cloned.1.call-start = ((), (), s32[]{:S(2)}) async-start(), calls=%async_computation.7 | async-start | bytes 262144 | tf_op jit(solution)/shard_map/psum | solution.py:40
Sparse Core Ops, SparseCore 0:
  34.5 45.8 all-reduce.8
  232.9 100.2 all-reduce.10
  382.5 43.3 all-reduce.12
  578.4 100.1 all-reduce.14
  727.7 43.4 all-reduce.16
  923.7 100.1 all-reduce.18
  1073.0 43.3 all-reduce.20
  1269.8 100.1 all-reduce.22
where the time goes:
time: 1430 us; the launch traced here: 1410 us
  waiting for transfers between devices  578 us (40%)
  blocking collectives  558 us (39%)
  matrix products  204 us (14%)
  other arithmetic  55 us (4%)
  between operations  14.6 us (1%)
    psum x4, blocking collectives, frame_space(): lower = jnp.linalg.cholesky(lax.psum(gram_matrix(block), 'space'))  493 us
    psum x4, waiting for transfers between devices, project(): return lax.psum(jnp.dot(basis, snapshots, precision=highest), 'space')  401 us
    psum x4, waiting for transfers between devices, new_basis(): return frame_space(lax.psum(partial_value, 'param'))  176 us
    dot_general x3, matrix products, shards(): lax.dot_general(column_frame, snapshots, (((1,), (1,)), ((), ())), precis...  79 us
    dot_general x4, matrix products, project(): return lax.psum(jnp.dot(basis, snapshots, precision=highest), 'space')  72.6 us
    psum x4, blocking collectives, frame_param(): lower = jnp.linalg.cholesky(lax.psum(gram_matrix(block), 'param'))  53.4 us
  transfers between devices with their start and end apart: 8, of which 8 were waited for; matrix products, arithmetic and copies ran while one was open for 0% of the time, Pallas kernels for 0%

commit v1 on v0

v1 whole, which is shorter than its diff:
```python
import functools
import math

import jax
import jax.numpy as jnp
from jax import lax
from jax.experimental import pallas as pl
from jax.experimental.pallas import tpu as pltpu
from jax.sharding import PartitionSpec as P

MESH = pl.DeviceIdType.MESH
R = 32
MODES = 256
ITERS = 3
F32, BF16 = jnp.float32, jnp.bfloat16
NN = (((1,), (0,)), ((), ()))
NT = (((1,), (1,)), ((), ()))


def exact(a, b, dims=NN):
    return lax.dot_general(a, b, dims, precision=lax.Precision.HIGHEST, preferred_element_type=F32)


def split(value):
    high = value.astype(BF16)
    low = (value - high.astype(F32)).astype(BF16)
    return jnp.concatenate([high, low], axis=0)


def fold(pair):
    return pair[:R] + pair[R:]


def gram_of(stacked):
    both = lax.dot_general(stacked, stacked, NT, preferred_element_type=F32)
    half = fold(both)
    return half[:, :R] + half[:, R:]


def inverse_factor(gram):
    rows = lax.broadcasted_iota(jnp.int32, (R, R), 0)
    columns = lax.broadcasted_iota(jnp.int32, (R, R), 1)
    eye = jnp.where(rows == columns, 1.0, 0.0).astype(F32)
    work = jnp.concatenate([gram, eye], axis=1)
    below = lax.broadcasted_iota(jnp.int32, (R, 2 * R), 0)
    for j in range(R - 1):
        row = work[j : j + 1, :]
        scaled = row / row[:, j : j + 1]
        work = work - jnp.where(below > j, work[:, j : j + 1], 0.0) * scaled
    diagonal = jnp.sum(jnp.where(rows == columns, work[:, :R], 0.0), axis=1, keepdims=True)
    return work[:, R:] / jnp.sqrt(diagonal)


def pack(square):
    return jnp.concatenate([square[8 * i : 8 * i + 8] for i in range(4)], axis=1)


def unpack(tile):
    return jnp.concatenate([tile[:, R * i : R * i + R] for i in range(4)], axis=0)


def kernel(
    ns, nx, total_rows, unfold_rows,
    snap, sketch, following, basis_out, second_out, rest_out,
    high, low, stage, zst, ypart, first_in, second_in, yfull, zacc, zfull,
    tiles_out, tiles_in, sums, gram_out, gram_in, last_out, last_in,
    factor_z, factor_y,
    load_sem, send_sem, recv_sem, tile_send, tile_recv, sum_send, sum_recv,
    gram_send, gram_recv, last_send, last_recv, out_sem,
):
    me, mx = lax.axis_index("space"), lax.axis_index("param")
    right, left, across = lax.rem(mx + 1, nx), lax.rem(mx + nx - 1, nx), lax.rem(mx + 2, nx)
    halves, hrows, columns = high.shape
    per = tiles_out.shape[1] - 1

    def part(quarter, half):
        return quarter * 2 + half

    order = [
        part(across, 0), part(across, 1), part(right, 1), part(left, 0),
        part(right, 0), part(left, 1), part(mx, 0), part(mx, 1),
    ]

    def load(n):
        return pltpu.make_async_copy(
            snap.at[pl.ds(pl.multiple_of(order[n] * hrows, 256), hrows), :],
            stage.at[n % 2], load_sem.at[n % 2],
        )

    load(0).start()
    load(1).start()

    barrier = pltpu.get_barrier_semaphore()

    def greet(d, carry):
        pl.semaphore_signal(barrier, inc=1, device_id=(lax.rem(me + d, ns), mx), device_id_type=MESH)
        return carry

    lax.fori_loop(1, ns, greet, 0)
    for d in range(1, nx):
        pl.semaphore_signal(barrier, inc=1, device_id=(me, lax.rem(mx + d, nx)), device_id_type=MESH)

    zst[...] = split(sketch[...].T)
    factor_z[...] = jnp.where(
        lax.broadcasted_iota(jnp.int32, (R, R), 0) == lax.broadcasted_iota(jnp.int32, (R, R), 1), 1.0, 0.0
    ).astype(F32)
    pl.semaphore_wait(barrier, ns - 1 + nx - 1)

    def compute(it, n):
        h = order[n]

        @pl.when(it == 0)
        def _():
            load(n).wait()

            def cut(i, carry):
                at = pl.ds(pl.multiple_of(i * 16, 16), 16)
                value = stage[n % 2, at, :]
                top = value.astype(BF16)
                high[h, at, :] = top
                low[h, at, :] = (value - top.astype(F32)).astype(BF16)
                return carry

            lax.fori_loop(0, hrows // 16, cut, 0)
            if n + 2 < halves:
                load(n + 2).start()

        for b in range(hrows // 256):
            at = pl.ds(b * 256, 256)
            pair = lax.dot_general(zst[...], high[h, at, :], NT, preferred_element_type=F32)
            pair += lax.dot_general(zst[...], low[h, at, :], NT, preferred_element_type=F32)
            ypart[h, :, at] = fold(pair)

    def along_x(source, target, n, it, x):
        return pltpu.make_async_remote_copy(
            src_ref=source, dst_ref=target, send_sem=send_sem.at[n], recv_sem=recv_sem.at[it, n],
            device_id=(me, x), device_id_type=MESH,
        )

    def accumulate(it, h):
        stacked = split(yfull[it, h])
        for b in range(columns // 256):
            at = pl.ds(b * 256, 256)
            pair = lax.dot_general(stacked, high[h, :, at], NN, preferred_element_type=F32)
            pair += lax.dot_general(stacked, low[h, :, at], NN, preferred_element_type=F32)
            zacc[:, at] += fold(pair)
        return gram_of(stacked)

    def gram_copy(it, d):
        return pltpu.make_async_remote_copy(
            src_ref=gram_out, dst_ref=gram_in.at[it, mx], send_sem=gram_send.at[d - 1], recv_sem=gram_recv.at[it, d - 1],
            device_id=(me, lax.rem(mx + d, nx)), device_id_type=MESH,
        )

    def iteration(it, carry):
        compute(it, 0)
        a_right = along_x(ypart.at[order[0]], first_in.at[it, 0], 0, it, right)
        a_right.start()
        compute(it, 1)
        a_left = along_x(ypart.at[order[1]], first_in.at[it, 1], 1, it, left)
        a_left.start()
        compute(it, 2)
        b_right = along_x(ypart.at[order[2]], second_in.at[it, 0, 1], 2, it, right)
        b_right.start()
        compute(it, 3)
        b_left = along_x(ypart.at[order[3]], second_in.at[it, 1, 0], 3, it, left)
        b_left.start()
        compute(it, 4)
        a_right.wait_recv()
        ypart[order[4]] += first_in[it, 0]
        c_right = along_x(ypart.at[order[4]], second_in.at[it, 0, 0], 4, it, right)
        c_right.start()
        compute(it, 5)
        a_left.wait_recv()
        ypart[order[5]] += first_in[it, 1]
        c_left = along_x(ypart.at[order[5]], second_in.at[it, 1, 1], 5, it, left)
        c_left.start()
        compute(it, 6)
        compute(it, 7)

        @pl.when(it > 0)
        def _():
            for d in range(1, nx):
                gram_copy(it - 1, d).wait()
            total = gram_in[it - 1, 0]
            for x in range(1, nx):
                total = total + gram_in[it - 1, x]
            factor_z[...] = inverse_factor(unpack(total))

        def finish(half):
            h = part(mx, half)
            value = ypart[h] + second_in[it, 0, half] + second_in[it, 1, half]
            yfull[it, h] = exact(factor_z[...], value)

        def to_right(h, n):
            return along_x(yfull.at[it, h], yfull.at[it, h], n, it, right)

        def to_left(h, n):
            return along_x(yfull.at[it, h], yfull.at[it, h], n, it, left)

        c_right.wait_recv()
        b_left.wait_recv()
        finish(0)
        own0_right = to_right(part(mx, 0), 6)
        own0_right.start()
        own0_left = to_left(part(mx, 0), 7)
        own0_left.start()
        b_right.wait_recv()
        c_left.wait_recv()
        finish(1)
        own1_left = to_left(part(mx, 1), 8)
        own1_left.start()
        own1_right = to_right(part(mx, 1), 9)
        own1_right.start()

        zacc[...] = jnp.zeros_like(zacc)
        gram = accumulate(it, part(mx, 0))
        gram = gram + accumulate(it, part(mx, 1))
        own0_right.wait_recv()
        on_right = to_right(part(left, 0), 10)
        on_right.start()
        own1_left.wait_recv()
        on_left = to_left(part(right, 1), 11)
        on_left.start()
        gram = gram + accumulate(it, part(left, 0))
        gram = gram + accumulate(it, part(right, 1))
        own0_left.wait_recv()
        gram = gram + accumulate(it, part(right, 0))
        own1_right.wait_recv()
        gram = gram + accumulate(it, part(left, 1))
        on_right.wait_recv()
        gram = gram + accumulate(it, part(across, 0))
        on_left.wait_recv()
        gram = gram + accumulate(it, part(across, 1))

        packed = pack(gram)
        for g in range(columns // 128):
            block = zacc[:, pl.ds(g * 128, 128)].reshape(4, 8, 128)
            for t in range(4):
                tiles_out[(g * 4 + t) // per, (g * 4 + t) % per] = block[t]

        def place(s, carry):
            tiles_out[s, per] = packed
            return carry

        lax.fori_loop(0, ns, place, 0)
        tiles_in[it, me] = tiles_out[me]

        def tile_copy(d):
            s = lax.rem(me + d, ns)
            return pltpu.make_async_remote_copy(
                src_ref=tiles_out.at[s], dst_ref=tiles_in.at[it, me], send_sem=tile_send, recv_sem=tile_recv.at[it],
                device_id=(s, mx), device_id_type=MESH,
            )

        def sum_copy(d):
            s = lax.rem(me + d, ns)
            return pltpu.make_async_remote_copy(
                src_ref=sums.at[it, me], dst_ref=sums.at[it, me], send_sem=sum_send, recv_sem=sum_recv.at[it],
                device_id=(s, mx), device_id_type=MESH,
            )

        def start(copy):
            def go(d, carry):
                copy(d).start()
                return carry

            lax.fori_loop(1, ns, go, 0)

        def all_but_one(ref, sem):
            some = ref.at[it, pl.ds(0, ns - 1)]
            pltpu.make_async_copy(some, some, sem).wait()

        start(tile_copy)
        for copy in (a_right, a_left, b_right, b_left, c_right, c_left):
            copy.wait_send()
        for copy in (own0_right, own0_left, own1_left, own1_right, on_right, on_left):
            copy.wait_send()
        all_but_one(tiles_in, tile_recv.at[it])

        def add(s, carry):
            return carry + tiles_in[it, s]

        total = lax.fori_loop(1, ns, add, tiles_in[it, 0])
        sums[it, me] = total[:per]
        start(sum_copy)
        factor_y[...] = inverse_factor(unpack(total[per]))
        all_but_one(tiles_in, tile_send)
        all_but_one(sums, sum_recv.at[it])
        all_but_one(sums, sum_send)
        gathered = sums[it].reshape(R, 8, 128)
        for g in range(columns // 128):
            block = gathered[g * 4 : g * 4 + 4].reshape(R, 128)
            zfull[:, g * 128 : g * 128 + 128] = exact(factor_y[...], block)

        @pl.when(it < ITERS)
        def _():
            stacked = split(zfull[...])
            zst[...] = stacked
            mine = pack(gram_of(stacked))
            gram_out[...] = mine
            gram_in[it, mx] = mine
            for d in range(1, nx):
                gram_copy(it, d).start()

        return carry

    lax.fori_loop(0, ITERS + 1, iteration, 0)

    turned = following[...].T
    slices = columns // MODES
    zfull[...] = zfull[...] * (1.0 / math.sqrt(total_rows))
    sketched, rest = [], jnp.zeros((R, MODES), F32)
    for i in range(slices):
        block = zfull[:, pl.ds(i * MODES, MODES)]
        one = exact(turned, block, NT)
        rest = rest + exact(one, block)
        sketched.append(one)
    sketched = jnp.concatenate(sketched, axis=1)
    last_out[:, pl.ds(0, MODES)] = rest
    last_out[:, pl.ds(MODES, 128)] = jnp.concatenate(
        [exact(sketched, sketched, NT), jnp.zeros((R, 128 - R), F32)], axis=1
    )
    last_in[mx] = last_out[...]

    def last_copy(d):
        return pltpu.make_async_remote_copy(
            src_ref=last_out, dst_ref=last_in.at[mx], send_sem=last_send.at[d - 1], recv_sem=last_recv.at[d - 1],
            device_id=(me, lax.rem(mx + d, nx)), device_id_type=MESH,
        )

    for d in range(1, nx):
        last_copy(d).start()

    def write(h):
        return pltpu.make_async_copy(
            ypart.at[h], basis_out.at[:, pl.ds(h * hrows, hrows)], out_sem.at[h]
        )

    for h in range(halves):
        ypart[h] = exact(factor_y[...], yfull[ITERS, h]) * math.sqrt(total_rows)
        write(h).start()

    for d in range(1, nx):
        last_copy(d).wait()
    total = last_in[0]
    for x in range(1, nx):
        total = total + last_in[x]
    factor = inverse_factor(total[:, MODES : MODES + R])
    second_out[...] = exact(factor, sketched) * math.sqrt(unfold_rows)
    rest_out[...] = exact(factor, total[:, :MODES]) / math.sqrt(unfold_rows)
    for h in range(halves):
        write(h).wait()


def solution(mesh):
    ns, nx = mesh.shape["space"], mesh.shape["param"]

    def shards(snapshots, sketch, following):
        rows, columns = snapshots.shape
        hrows = rows // (2 * nx)
        per = R // ns
        slices = columns // MODES
        steps = ITERS + 1
        dma = pltpu.SemaphoreType.DMA
        return pl.pallas_call(
            functools.partial(kernel, ns, nx, rows * ns, slices * R * nx),
            out_shape=(
                jax.ShapeDtypeStruct((R, rows), F32),
                jax.ShapeDtypeStruct((R, slices * R), F32),
                jax.ShapeDtypeStruct((R, MODES), F32),
            ),
            in_specs=[
                pl.BlockSpec(memory_space=pl.ANY),
                pl.BlockSpec(memory_space=pltpu.VMEM),
                pl.BlockSpec(memory_space=pltpu.VMEM),
            ],
            out_specs=(
                pl.BlockSpec(memory_space=pl.ANY),
                pl.BlockSpec(memory_space=pltpu.VMEM),
                pl.BlockSpec(memory_space=pltpu.VMEM),
            ),
            scratch_shapes=[
                pltpu.VMEM((2 * nx, hrows, columns), BF16),
                pltpu.VMEM((2 * nx, hrows, columns), BF16),
                pltpu.VMEM((2, hrows, columns), F32),
                pltpu.VMEM((2 * R, columns), BF16),
                pltpu.VMEM((2 * nx, R, hrows), F32),
                pltpu.VMEM((steps, 2, R, hrows), F32),
                pltpu.VMEM((steps, 2, 2, R, hrows), F32),
                pltpu.VMEM((steps, 2 * nx, R, hrows), F32),
                pltpu.VMEM((R, columns), F32),
                pltpu.VMEM((R, columns), F32),
                pltpu.VMEM((ns, per + 1, 8, 128), F32),
                pltpu.VMEM((steps, ns, per + 1, 8, 128), F32),
                pltpu.VMEM((steps, ns, per, 8, 128), F32),
                pltpu.VMEM((8, 128), F32),
                pltpu.VMEM((steps, nx, 8, 128), F32),
                pltpu.VMEM((R, MODES + 128), F32),
                pltpu.VMEM((nx, R, MODES + 128), F32),
                pltpu.VMEM((R, R), F32),
                pltpu.VMEM((R, R), F32),
                dma((2,)),
                dma((12,)),
                dma((steps, 12)),
                dma,
                dma((steps,)),
                dma,
                dma((steps,)),
                dma((nx - 1,)),
                dma((steps, nx - 1)),
                dma((nx - 1,)),
                dma((nx - 1,)),
                dma((2 * nx,)),
            ],
            compiler_params=pltpu.CompilerParams(
                collective_id=0, has_side_effects=True, vmem_limit_bytes=60 * 1024 * 1024
            ),
        )(snapshots, sketch, following)

    return jax.shard_map(
        shards,
        mesh=mesh,
        in_specs=(P("space", "param"), P("param", None), P()),
        out_specs=(P(None, "space"), P(None, "param"), P()),
        check_vma=False,
    )
```

time: 1430 us -> 177 us (0.12); the launches traced: 1410 us -> 177 us
  waiting for transfers between devices: 578 us -> 0 us
  blocking collectives: 558 us -> 0 us
  matrix products: 204 us -> 0 us
  Pallas kernels: 0 us -> 168 us
  other arithmetic: 55 us -> 0 us
    psum x8 -> x0, waiting for transfers between devices: 578 us -> none  [the longest x4 401 us: project(): return lax.psum(jnp.dot(basis, snapshots, precision=highest), 'space')]
    psum x9 -> x0, blocking collectives: 558 us -> none  [the longest x4 493 us: frame_space(): lower = jnp.linalg.cholesky(lax.psum(gram_matrix(block), 'space'))]
    dot_general x18 -> x0, matrix products: 191 us -> none  [the longest x3 79 us: shards(): lax.dot_general(column_frame, snapshots, (((1,), (1,)), ((), ())), precis...]
    pallas_call x0 -> x1, Pallas kernels: none -> 168 us  [shards(): pl.pallas_call(functools.partial(kernel, ns, nx, rows * ns, slices * R *...]
    another operation x40 -> x0, other arithmetic: 53.4 us -> none  [the longest x16 24.7 us: apply_factor(): return jax.scipy.linalg.solve_triangular(lower, block, lower=True)]
  transfers between devices with their start and end apart: 8 -> 0, of which waited for: 8 -> 0; matrix products, arithmetic and copies ran while one was open for 0% -> 0% of each run, Pallas kernels for 0% -> 0%
where the time goes in v1:
time: 177 us
  Pallas kernels  168 us (95%)
  local copies, waits for them, and re-layouts  8.19 us (5%)
    pallas_call x1, Pallas kernels, shards(): pl.pallas_call(functools.partial(kernel, ns, nx, rows * ns, slices * R *...  168 us
    unnamed x5, local copies, waits for them, and re-layouts  8.19 us

profile of v1, /device:TPU:1, one launch (start us, length us, event | category | flops | bytes accessed | tf_op | source)
XLA Modules:
  0.0 176.5 jit_solution(11129149045809892928)
XLA Ops:
  0.6 1.5 copy.7.following
  2.2 1.9 %copy.6.sketch = f32[1024,32]{1,0:T(8,128)} copy(f32[1024,32]{0,1:T(8,128)} %param.4) | data formatting | bytes 262144 | tf_op args[1]
  4.1 167.7 %shard_map.58 = (f32[32,6144]{1,0:T(8,128)}, f32[32,128]{1,0:T(8,128)}, f32[32,256]{1,0:T(8,128)}) custom-call(f32[6144,1024]{1,0:T(8,128)} %snap.1, f32[1024,32]{1,0:T(8,128)} %copy.6.sketch, f32[256,32]{1,0:T(8,128)} %copy.7.following), custom_call_target="tpu_custom_call" | custom-call | tf_op jit(solution)/shard_map/pallas_call | solution.py:366
  171.8 2.1 %copy.11 = f32[32,6144]{1,0:T(8,128)} copy(f32[32,6144]{1,0:T(8,128)} %get-tuple-element.6) | data formatting | bytes 1572864
  173.8 1.3 copy.12
  175.2 1.4 copy.13

commit v2 on v1

v2 whole, which is shorter than its diff:
```python
import functools
import math

import jax
import jax.numpy as jnp
from jax import lax
from jax.experimental import pallas as pl
from jax.experimental.pallas import tpu as pltpu
from jax.sharding import PartitionSpec as P

MESH = pl.DeviceIdType.MESH
R = 32
MODES = 256
ITERS = 3
PIECES = 6
F32, BF16 = jnp.float32, jnp.bfloat16
NN = (((1,), (0,)), ((), ()))
NT = (((1,), (1,)), ((), ()))


def exact(a, b, dims=NN):
    return lax.dot_general(a, b, dims, precision=lax.Precision.HIGHEST, preferred_element_type=F32)


def split(value):
    high = value.astype(BF16)
    low = (value - high.astype(F32)).astype(BF16)
    return jnp.concatenate([high, low], axis=0)


def fold(pair):
    return pair[:R] + pair[R:]


def gram_of(stacked):
    both = lax.dot_general(stacked, stacked, NT, preferred_element_type=F32)
    half = fold(both)
    return half[:, :R] + half[:, R:]


def inverse_factor(gram):
    rows = lax.broadcasted_iota(jnp.int32, (R, R), 0)
    columns = lax.broadcasted_iota(jnp.int32, (R, R), 1)
    eye = jnp.where(rows == columns, 1.0, 0.0).astype(F32)
    work = jnp.concatenate([gram, eye], axis=1)
    below = lax.broadcasted_iota(jnp.int32, (R, 2 * R), 0)
    for j in range(R - 1):
        row = work[j : j + 1, :]
        scaled = row / row[:, j : j + 1]
        work = work - jnp.where(below > j, work[:, j : j + 1], 0.0) * scaled
    diagonal = jnp.sum(jnp.where(rows == columns, work[:, :R], 0.0), axis=1, keepdims=True)
    return work[:, R:] / jnp.sqrt(diagonal)


def pack(square):
    return jnp.concatenate([square[8 * i : 8 * i + 8] for i in range(4)], axis=1)


def unpack(tile):
    return jnp.concatenate([tile[:, R * i : R * i + R] for i in range(4)], axis=0)


def kernel(
    ns, nx, total_rows, unfold_rows,
    snap, sketch, following, basis_out, second_out, rest_out,
    high, low, stage, zst, ypart, first_in, second_in, yfull, zacc, zfull,
    tiles_out, tiles_in, sums, gram_in, own_in, space_in, last_out, last_in,
    factor_z, factor_y,
    load_sem, send_sem, recv_sem, tile_send, tile_recv, sum_send, sum_recv,
    gram_send, gram_recv, own_send, own_recv, space_send, space_recv, last_send, last_recv, out_sem,
):
    me, mx = lax.axis_index("space"), lax.axis_index("param")
    right, left, across = lax.rem(mx + 1, nx), lax.rem(mx + nx - 1, nx), lax.rem(mx + 2, nx)
    pieces, prows, columns = high.shape
    per = tiles_out.shape[1]
    third = PIECES // 2
    loads = stage.shape[0]

    def part(quarter, piece):
        return quarter * PIECES + piece

    steps = range(third)
    far = [part(across, k + side * third) for k in steps for side in (0, 1)]
    plain = [h for k in steps for h in (part(right, k + third), part(left, k))]
    merged = [h for k in steps for h in (part(right, k), part(left, k + third))]
    own = [part(mx, k + side * third) for k in steps for side in (0, 1)]
    order = far + plain + merged + own

    def load(n):
        return pltpu.make_async_copy(
            snap.at[pl.ds(pl.multiple_of(order[n] * prows, prows), prows), :],
            stage.at[n % loads], load_sem.at[n % loads],
        )

    for n in range(loads):
        load(n).start()

    barrier = pltpu.get_barrier_semaphore()

    def greet(d, carry):
        pl.semaphore_signal(barrier, inc=1, device_id=(lax.rem(me + d, ns), mx), device_id_type=MESH)
        return carry

    lax.fori_loop(1, ns, greet, 0)
    for d in range(1, nx):
        pl.semaphore_signal(barrier, inc=1, device_id=(me, lax.rem(mx + d, nx)), device_id_type=MESH)

    zst[...] = split(sketch[...])
    eye = jnp.where(
        lax.broadcasted_iota(jnp.int32, (R, R), 0) == lax.broadcasted_iota(jnp.int32, (R, R), 1), 1.0, 0.0
    ).astype(F32)
    for x in range(nx):
        gram_in[0, x] = pack(eye * (1.0 / nx))
    pl.semaphore_wait(barrier, ns - 1 + nx - 1)

    def fetch(n):
        load(n).wait()

        def cut(i, carry):
            at = pl.ds(pl.multiple_of(i * 16, 16), 16)
            value = stage[n % loads, at, :]
            top = value.astype(BF16)
            high[order[n], at, :] = top
            low[order[n], at, :] = (value - top.astype(F32)).astype(BF16)
            return carry

        lax.fori_loop(0, prows // 16, cut, 0)
        if n + loads < pieces:
            load(n + loads).start()

    def product(n):
        h = order[n]
        pair = lax.dot_general(zst[...], high[h], NT, preferred_element_type=F32)
        pair += lax.dot_general(zst[...], low[h], NT, preferred_element_type=F32)
        return fold(pair)

    def compute(it, n):
        pl.when(it == 0)(lambda: fetch(n))
        ypart[order[n]] = product(n)

    def along_x(source, target, n, it, x):
        return pltpu.make_async_remote_copy(
            src_ref=source, dst_ref=target, send_sem=send_sem.at[n], recv_sem=recv_sem.at[it, n],
            device_id=(me, x), device_id_type=MESH,
        )

    def accumulate(it, some):
        stacked = [split(yfull[it, h]) for h in some]
        for b in range(columns // 256):
            at = pl.ds(b * 256, 256)
            pair = None
            for a, h in zip(stacked, some):
                one = lax.dot_general(a, high[h, :, at], NN, preferred_element_type=F32)
                one += lax.dot_general(a, low[h, :, at], NN, preferred_element_type=F32)
                pair = one if pair is None else pair + one
            zacc[:, at] += fold(pair)
        return stacked

    def peer_copy(ref, it, d, send, recv):
        return pltpu.make_async_remote_copy(
            src_ref=ref.at[it, mx], dst_ref=ref.at[it, mx], send_sem=send.at[d - 1], recv_sem=recv.at[it, d - 1],
            device_id=(me, lax.rem(mx + d, nx)), device_id_type=MESH,
        )

    def space_copy(source, ref, it, d, send, recv):
        s = lax.rem(me + d, ns)
        return pltpu.make_async_remote_copy(
            src_ref=source(s), dst_ref=ref.at[it, me], send_sem=send, recv_sem=recv.at[it],
            device_id=(s, mx), device_id_type=MESH,
        )

    def start_space(source, ref, it, send, recv):
        def go(d, carry):
            space_copy(source, ref, it, d, send, recv).start()
            return carry

        lax.fori_loop(1, ns, go, 0)

    def all_but_one(ref, it, sem):
        some = ref.at[it, pl.ds(0, ns - 1)]
        pltpu.make_async_copy(some, some, sem).wait()

    def sum_of(ref, it, count):
        total = ref[it, 0]
        for x in range(1, count):
            total = total + ref[it, x]
        return total

    def iteration(it, carry):
        far_copies, plain_copies, merged_copies = [], [], []
        for n, h in enumerate(far):
            k, side = divmod(n, 2)
            compute(it, n)
            copy = along_x(ypart.at[h], first_in.at[it, side, k], n, it, left if side else right)
            copy.start()
            far_copies.append(copy)
        for m, h in enumerate(plain):
            k, side = divmod(m, 2)
            n = len(far) + m
            compute(it, n)
            slot = second_in.at[it, side, k if side else k + third]
            copy = along_x(ypart.at[h], slot, n, it, left if side else right)
            copy.start()
            plain_copies.append(copy)
        for m, h in enumerate(merged):
            k, side = divmod(m, 2)
            n = len(far) + len(plain) + m
            compute(it, n)
            far_copies[m].wait_recv()
            ypart[h] += first_in[it, side, k]
            slot = second_in.at[it, side, k + third if side else k]
            copy = along_x(ypart.at[h], slot, n, it, left if side else right)
            copy.start()
            merged_copies.append(copy)

        base = pieces - len(own)

        @pl.when(it == 0)
        def _():
            for m in range(len(own)):
                fetch(base + m)

        @pl.when(it > 0)
        def _():
            for d in range(1, nx):
                peer_copy(gram_in, it, d, gram_send, gram_recv).wait()

        factor = inverse_factor(unpack(sum_of(gram_in, it, nx)))
        for m, h in enumerate(own):
            ypart[h] = product(base + m)
        factor_z[...] = factor

        spread = []

        def send_own(h, n, x):
            copy = along_x(yfull.at[it, h], yfull.at[it, h], n, it, x)
            copy.start()
            spread.append(copy)
            return copy

        straight = []
        for m, h in enumerate(own):
            k, side = divmod(m, 2)
            piece = k + side * third
            merged_copies[2 * k + side].wait_recv()
            plain_copies[2 * k + 1 - side].wait_recv()
            value = ypart[h] + second_in[it, 0, piece] + second_in[it, 1, piece]
            yfull[it, h] = exact(factor_z[...], value)
            straight.append(send_own(h, 18 + m, left if side else right))
        turned = []
        for m, h in enumerate(own):
            turned.append(send_own(h, 24 + m, right if m % 2 else left))

        zacc[...] = jnp.zeros_like(zacc)
        stacked = accumulate(it, own)
        gram = sum(gram_of(a) for a in stacked)
        own_in[it, mx] = pack(gram)
        for d in range(1, nx):
            peer_copy(own_in, it, d, own_send, own_recv).start()
        onward = []
        for k in steps:
            straight[2 * k].wait_recv()
            onward.append(send_own(part(left, k), 30 + 2 * k, right))
            straight[2 * k + 1].wait_recv()
            onward.append(send_own(part(right, k + third), 31 + 2 * k, left))
            accumulate(it, [part(left, k), part(right, k + third)])

        for d in range(1, nx):
            peer_copy(own_in, it, d, own_send, own_recv).wait()
        space_in[it, me] = sum_of(own_in, it, nx)
        start_space(lambda s: space_in.at[it, me], space_in, it, space_send, space_recv)

        for k in steps:
            turned[2 * k].wait_recv()
            turned[2 * k + 1].wait_recv()
            accumulate(it, [part(right, k), part(left, k + third)])
        for k in steps:
            onward[2 * k].wait_recv()
            onward[2 * k + 1].wait_recv()
            accumulate(it, [part(across, k), part(across, k + third)])

        for g in range(columns // 128):
            block = zacc[:, pl.ds(g * 128, 128)].reshape(4, 8, 128)
            for t in range(4):
                tiles_out[(g * 4 + t) // per, (g * 4 + t) % per] = block[t]
        start_space(lambda s: tiles_out.at[s], tiles_in, it, tile_send, tile_recv)
        tiles_in[it, me] = tiles_out[me]

        all_but_one(space_in, it, space_recv.at[it])
        factor_y[...] = inverse_factor(unpack(sum_of(space_in, it, ns)))
        all_but_one(space_in, it, space_send)
        for copy in far_copies + plain_copies + merged_copies + spread:
            copy.wait_send()

        all_but_one(tiles_in, it, tile_recv.at[it])
        sums[it, me] = sum_of(tiles_in, it, ns)
        start_space(lambda s: sums.at[it, me], sums, it, sum_send, sum_recv)
        all_but_one(tiles_in, it, tile_send)
        all_but_one(sums, it, sum_recv.at[it])
        gathered = sums[it].reshape(R, 8, 128)
        for g in range(columns // 128):
            block = gathered[g * 4 : g * 4 + 4].reshape(R, 128)
            zfull[:, g * 128 : g * 128 + 128] = exact(factor_y[...], block)

        @pl.when(it < ITERS)
        def _():
            stacked = split(zfull[...])
            zst[...] = stacked
            gram_in[it + 1, mx] = pack(gram_of(stacked))
            for d in range(1, nx):
                peer_copy(gram_in, it + 1, d, gram_send, gram_recv).start()

        all_but_one(sums, it, sum_send)
        return carry

    lax.fori_loop(0, ITERS + 1, iteration, 0)

    slices = columns // MODES
    zfull[...] = zfull[...] * (1.0 / math.sqrt(total_rows))
    sketched, rest = [], jnp.zeros((R, MODES), F32)
    for i in range(slices):
        block = zfull[:, pl.ds(i * MODES, MODES)]
        one = exact(following[...], block, NT)
        rest = rest + exact(one, block)
        sketched.append(one)
    sketched = jnp.concatenate(sketched, axis=1)
    last_out[:, pl.ds(0, MODES)] = rest
    last_out[:, pl.ds(MODES, 128)] = jnp.concatenate(
        [exact(sketched, sketched, NT), jnp.zeros((R, 128 - R), F32)], axis=1
    )
    last_in[mx] = last_out[...]

    def last_copy(d):
        return pltpu.make_async_remote_copy(
            src_ref=last_out, dst_ref=last_in.at[mx], send_sem=last_send.at[d - 1], recv_sem=last_recv.at[d - 1],
            device_id=(me, lax.rem(mx + d, nx)), device_id_type=MESH,
        )

    for d in range(1, nx):
        last_copy(d).start()

    def write(h):
        return pltpu.make_async_copy(
            ypart.at[h], basis_out.at[:, pl.ds(h * prows, prows)], out_sem.at[h]
        )

    for h in range(pieces):
        ypart[h] = exact(factor_y[...], yfull[ITERS, h]) * math.sqrt(total_rows)
        write(h).start()

    for d in range(1, nx):
        last_copy(d).wait()
    total = last_in[0]
    for x in range(1, nx):
        total = total + last_in[x]
    factor = inverse_factor(total[:, MODES : MODES + R])
    second_out[...] = exact(factor, sketched) * math.sqrt(unfold_rows)
    rest_out[...] = exact(factor, total[:, :MODES]) / math.sqrt(unfold_rows)
    for h in range(pieces):
        write(h).wait()


def solution(mesh):
    ns, nx = mesh.shape["space"], mesh.shape["param"]

    def shards(snapshots, sketch, following):
        rows, columns = snapshots.shape
        pieces = PIECES * nx
        prows = rows // pieces
        per = R // ns
        slices = columns // MODES
        steps = ITERS + 1
        dma = pltpu.SemaphoreType.DMA
        return pl.pallas_call(
            functools.partial(kernel, ns, nx, rows * ns, slices * R * nx),
            out_shape=(
                jax.ShapeDtypeStruct((R, rows), F32),
                jax.ShapeDtypeStruct((R, slices * R), F32),
                jax.ShapeDtypeStruct((R, MODES), F32),
            ),
            in_specs=[
                pl.BlockSpec(memory_space=pl.ANY),
                pl.BlockSpec(memory_space=pltpu.VMEM),
                pl.BlockSpec(memory_space=pltpu.VMEM),
            ],
            out_specs=(
                pl.BlockSpec(memory_space=pl.ANY),
                pl.BlockSpec(memory_space=pltpu.VMEM),
                pl.BlockSpec(memory_space=pltpu.VMEM),
            ),
            scratch_shapes=[
                pltpu.VMEM((pieces, prows, columns), BF16),
                pltpu.VMEM((pieces, prows, columns), BF16),
                pltpu.VMEM((4, prows, columns), F32),
                pltpu.VMEM((2 * R, columns), BF16),
                pltpu.VMEM((pieces, R, prows), F32),
                pltpu.VMEM((steps, 2, PIECES // 2, R, prows), F32),
                pltpu.VMEM((steps, 2, PIECES, R, prows), F32),
                pltpu.VMEM((steps, pieces, R, prows), F32),
                pltpu.VMEM((R, columns), F32),
                pltpu.VMEM((R, columns), F32),
                pltpu.VMEM((ns, per, 8, 128), F32),
                pltpu.VMEM((steps, ns, per, 8, 128), F32),
                pltpu.VMEM((steps, ns, per, 8, 128), F32),
                pltpu.VMEM((steps, nx, 8, 128), F32),
                pltpu.VMEM((steps, nx, 8, 128), F32),
                pltpu.VMEM((steps, ns, 8, 128), F32),
                pltpu.VMEM((R, MODES + 128), F32),
                pltpu.VMEM((nx, R, MODES + 128), F32),
                pltpu.VMEM((R, R), F32),
                pltpu.VMEM((R, R), F32),
                dma((4,)),
                dma((36,)),
                dma((steps, 36)),
                dma,
                dma((steps,)),
                dma,
                dma((steps,)),
                dma((nx - 1,)),
                dma((steps, nx - 1)),
                dma((nx - 1,)),
                dma((steps, nx - 1)),
                dma,
                dma((steps,)),
                dma((nx - 1,)),
                dma((nx - 1,)),
                dma((pieces,)),
            ],
            compiler_params=pltpu.CompilerParams(
                collective_id=0, has_side_effects=True, vmem_limit_bytes=60 * 1024 * 1024
            ),
        )(snapshots, sketch.T, following.T)

    return jax.shard_map(
        shards,
        mesh=mesh,
        in_specs=(P("space", "param"), P("param", None), P()),
        out_specs=(P(None, "space"), P(None, "param"), P()),
        check_vma=False,
    )
```

time: 177 us -> 180 us (1.017)
  Pallas kernels: 168 us -> 174 us
  local copies, waits for them, and re-layouts: 8.19 us -> 4.76 us
    pallas_call x1, Pallas kernels: 168 us -> 174 us  [shards(): pl.pallas_call(functools.partial(kernel, ns, nx, rows * ns, slices * R *...]
    unnamed x5 -> x3, local copies, waits for them, and re-layouts: 8.19 us -> 4.76 us
where the time goes in v2:
time: 180 us
  Pallas kernels  174 us (97%)
  local copies, waits for them, and re-layouts  4.76 us (3%)
    pallas_call x1, Pallas kernels, shards(): pl.pallas_call(functools.partial(kernel, ns, nx, rows * ns, slices * R *...  174 us
    unnamed x3, local copies, waits for them, and re-layouts  4.76 us

profile of v2, /device:TPU:1, one launch (start us, length us, event | category | flops | bytes accessed | tf_op | source)
XLA Modules:
  0.0 179.9 jit_solution(16722327878046271902)
XLA Ops:
  0.6 174.5 %shard_map.58 = (f32[32,6144]{1,0:T(8,128)}, f32[32,128]{1,0:T(8,128)}, f32[32,256]{1,0:T(8,128)}) custom-call(f32[6144,1024]{1,0:T(8,128)} %snap.1, f32[32,1024]{1,0:T(8,128)} %bitcast.2, f32[32,256]{1,0:T(8,128)} %bitcast.3), custom_call_target="tpu_custom_call" | custom-call | tf_op jit(solution)/shard_map/pallas_call | solution.py:374
  175.1 2.1 %copy.9 = f32[32,6144]{1,0:T(8,128)} copy(f32[32,6144]{1,0:T(8,128)} %get-tuple-element.6) | data formatting | bytes 1572864
  177.2 1.3 copy.10
  178.5 1.4 copy.11

commit v3 on v2

--- a/solution.py
+++ b/solution.py
@@ -63,9 +63,9 @@
 def kernel(
     ns, nx, total_rows, unfold_rows,
     snap, sketch, following, basis_out, second_out, rest_out,
-    high, low, stage, zst, ypart, first_in, second_in, yfull, zacc, zfull,
+    high, low, high_t, low_t, stage, zst, ypart, first_in, second_in, yfull, zacc, zfull,
     tiles_out, tiles_in, sums, gram_in, own_in, space_in, last_out, last_in,
-    factor_z, factor_y,
+    factor_y,
     load_sem, send_sem, recv_sem, tile_send, tile_recv, sum_send, sum_recv,
     gram_send, gram_recv, own_send, own_recv, space_send, space_recv, last_send, last_recv, out_sem,
 ):
@@ -85,6 +85,9 @@
     merged = [h for k in steps for h in (part(right, k), part(left, k + third))]
     own = [part(mx, k + side * third) for k in steps for side in (0, 1)]
     order = far + plain + merged + own
+    quarters = [across] * 6 + [right, left] * 6 + [mx] * 6
+    sides = [0, 1] * third + [1, 0] * third + [0, 1] * third * 2
+    places = [(quarters[n] * 2 + sides[n], n % 6 // 2) for n in range(4 * PIECES)]
 
     def load(n):
         return pltpu.make_async_copy(
@@ -106,11 +109,6 @@
         pl.semaphore_signal(barrier, inc=1, device_id=(me, lax.rem(mx + d, nx)), device_id_type=MESH)
 
     zst[...] = split(sketch[...])
-    eye = jnp.where(
-        lax.broadcasted_iota(jnp.int32, (R, R), 0) == lax.broadcasted_iota(jnp.int32, (R, R), 1), 1.0, 0.0
-    ).astype(F32)
-    for x in range(nx):
-        gram_in[0, x] = pack(eye * (1.0 / nx))
     pl.semaphore_wait(barrier, ns - 1 + nx - 1)
 
     def fetch(n):
@@ -128,15 +126,38 @@
         if n + loads < pieces:
             load(n + loads).start()
 
-    def product(n):
+    def product(n, first):
         h = order[n]
-        pair = lax.dot_general(zst[...], high[h], NT, preferred_element_type=F32)
-        pair += lax.dot_general(zst[...], low[h], NT, preferred_element_type=F32)
+        if first:
+            pair = lax.dot_general(zst[...], high[h], NT, preferred_element_type=F32)
+            pair += lax.dot_general(zst[...], low[h], NT, preferred_element_type=F32)
+        else:
+            side, k = places[n]
+            at = pl.ds(k * prows, prows)
+            pair = lax.dot_general(zst[...], high_t[side, :, at], NN, preferred_element_type=F32)
+            pair += lax.dot_general(zst[...], low_t[side, :, at], NN, preferred_element_type=F32)
         return fold(pair)
 
-    def compute(it, n):
-        pl.when(it == 0)(lambda: fetch(n))
-        ypart[order[n]] = product(n)
+    def turn(source, target):
+        def one(i, carry):
+            for b in range(columns // 256):
+                at = pl.ds(b * 256, 256)
+                rows = [source[i * third + k, :, at] for k in steps]
+                target[i, at, :] = jnp.concatenate(rows, axis=0).T
+            return carry
+
+        lax.fori_loop(0, pieces // third, one, 0)
+
+    def in_turn(numbers, first, ready):
+        ahead = None
+        for n in numbers:
+            if first:
+                fetch(n)
+            value = product(n, first)
+            if ahead is not None:
+                ready(*ahead)
+            ahead = (n, value)
+        ready(*ahead)
 
     def along_x(source, target, n, it, x):
         return pltpu.make_async_remote_copy(
@@ -162,19 +183,24 @@
             device_id=(me, lax.rem(mx + d, nx)), device_id_type=MESH,
         )
 
-    def space_copy(source, ref, it, d, send, recv):
-        s = lax.rem(me + d, ns)
-        return pltpu.make_async_remote_copy(
-            src_ref=source(s), dst_ref=ref.at[it, me], send_sem=send, recv_sem=recv.at[it],
-            device_id=(s, mx), device_id_type=MESH,
-        )
+    nc = 2
+    nz = min(4, ns // nc)
+    ny = ns // (nc * nz)
+    myy, myz, myc = me // (nz * nc), me // nc % nz, me % nc
+    hops = sorted(
+        (-min(dy, ny - dy) - min(dz, nz - dz), dy, dz, dc)
+        for dy in range(ny) for dz in range(nz) for dc in range(nc) if dy or dz or dc
+    )
+    others = [
+        ((lax.rem(myy + dy, ny) * nz + lax.rem(myz + dz, nz)) * nc + lax.rem(myc + dc, nc)) for _, dy, dz, dc in hops
+    ]
 
     def start_space(source, ref, it, send, recv):
-        def go(d, carry):
-            space_copy(source, ref, it, d, send, recv).start()
-            return carry
-
-        lax.fori_loop(1, ns, go, 0)
+        for s in others:
+            pltpu.make_async_remote_copy(
+                src_ref=source(s), dst_ref=ref.at[it, me], send_sem=send, recv_sem=recv.at[it],
+                device_id=(s, mx), device_id_type=MESH,
+            ).start()
 
     def all_but_one(ref, it, sem):
         some = ref.at[it, pl.ds(0, ns - 1)]
@@ -186,75 +212,78 @@
             total = total + ref[it, x]
         return total
 
-    def iteration(it, carry):
+    def iteration(it, first):
+        now = it % 2
         far_copies, plain_copies, merged_copies = [], [], []
-        for n, h in enumerate(far):
+
+        def send_far(n, value):
             k, side = divmod(n, 2)
-            compute(it, n)
-            copy = along_x(ypart.at[h], first_in.at[it, side, k], n, it, left if side else right)
+            ypart[order[n]] = value
+            copy = along_x(ypart.at[order[n]], first_in.at[now, side, k], n, it, left if side else right)
             copy.start()
             far_copies.append(copy)
-        for m, h in enumerate(plain):
-            k, side = divmod(m, 2)
-            n = len(far) + m
-            compute(it, n)
-            slot = second_in.at[it, side, k if side else k + third]
-            copy = along_x(ypart.at[h], slot, n, it, left if side else right)
+
+        def send_plain(n, value):
+            k, side = divmod(n - len(far), 2)
+            ypart[order[n]] = value
+            slot = second_in.at[now, side, k if side else k + third]
+            copy = along_x(ypart.at[order[n]], slot, n, it, left if side else right)
             copy.start()
             plain_copies.append(copy)
+
+        def send(n, value):
+            (send_far if n < len(far) else send_plain)(n, value)
+
+        def keep(n, value):
+            ypart[order[n]] = value
+
+        begun, base = len(far) + len(plain), pieces - len(own)
+        in_turn(range(begun), first, send)
+        in_turn(range(begun, base), first, keep)
         for m, h in enumerate(merged):
             k, side = divmod(m, 2)
-            n = len(far) + len(plain) + m
-            compute(it, n)
             far_copies[m].wait_recv()
-            ypart[h] += first_in[it, side, k]
-            slot = second_in.at[it, side, k + third if side else k]
-            copy = along_x(ypart.at[h], slot, n, it, left if side else right)
+            ypart[h] += first_in[now, side, k]
+            slot = second_in.at[now, side, k + third if side else k]
+            copy = along_x(ypart.at[h], slot, begun + m, it, left if side else right)
             copy.start()
             merged_copies.append(copy)
 
-        base = pieces - len(own)
-
-        @pl.when(it == 0)
-        def _():
-            for m in range(len(own)):
-                fetch(base + m)
-
-        @pl.when(it > 0)
-        def _():
+        if first:
+            factor = None
+        else:
             for d in range(1, nx):
                 peer_copy(gram_in, it, d, gram_send, gram_recv).wait()
-
-        factor = inverse_factor(unpack(sum_of(gram_in, it, nx)))
-        for m, h in enumerate(own):
-            ypart[h] = product(base + m)
-        factor_z[...] = factor
+            factor = inverse_factor(unpack(sum_of(gram_in, it, nx)))
+        in_turn(range(base, pieces), first, keep)
 
         spread = []
 
         def send_own(h, n, x):
-            copy = along_x(yfull.at[it, h], yfull.at[it, h], n, it, x)
+            copy = along_x(yfull.at[now, h], yfull.at[now, h], n, it, x)
             copy.start()
             spread.append(copy)
             return copy
 
-        straight = []
+        for copy in merged_copies + plain_copies:
+            copy.wait_recv()
+        value = jnp.concatenate(
+            [
+                ypart[h] + second_in[now, 0, m // 2 + m % 2 * third] + second_in[now, 1, m // 2 + m % 2 * third]
+                for m, h in enumerate(own)
+            ],
+            axis=1,
+        )
+        if factor is not None:
+            value = exact(factor, value)
         for m, h in enumerate(own):
-            k, side = divmod(m, 2)
-            piece = k + side * third
-            merged_copies[2 * k + side].wait_recv()
-            plain_copies[2 * k + 1 - side].wait_recv()
-            value = ypart[h] + second_in[it, 0, piece] + second_in[it, 1, piece]
-            yfull[it, h] = exact(factor_z[...], value)
-            straight.append(send_own(h, 18 + m, left if side else right))
-        turned = []
-        for m, h in enumerate(own):
-            turned.append(send_own(h, 24 + m, right if m % 2 else left))
+            yfull[now, h] = value[:, m * prows : (m + 1) * prows]
+        straight = [send_own(h, 18 + m, left if m % 2 else right) for m, h in enumerate(own)]
+        turned = [send_own(h, 24 + m, right if m % 2 else left) for m, h in enumerate(own)]
 
         zacc[...] = jnp.zeros_like(zacc)
-        stacked = accumulate(it, own)
-        gram = sum(gram_of(a) for a in stacked)
-        own_in[it, mx] = pack(gram)
+        accumulate(now, own)
+        own_in[it, mx] = pack(gram_of(split(value)))
         for d in range(1, nx):
             peer_copy(own_in, it, d, own_send, own_recv).start()
         onward = []
@@ -263,21 +292,21 @@
             onward.append(send_own(part(left, k), 30 + 2 * k, right))
             straight[2 * k + 1].wait_recv()
             onward.append(send_own(part(right, k + third), 31 + 2 * k, left))
-            accumulate(it, [part(left, k), part(right, k + third)])
+        accumulate(now, [h for k in steps for h in (part(left, k), part(right, k + third))])
 
         for d in range(1, nx):
             peer_copy(own_in, it, d, own_send, own_recv).wait()
         space_in[it, me] = sum_of(own_in, it, nx)
         start_space(lambda s: space_in.at[it, me], space_in, it, space_send, space_recv)
 
-        for k in steps:
-            turned[2 * k].wait_recv()
-            turned[2 * k + 1].wait_recv()
-            accumulate(it, [part(right, k), part(left, k + third)])
-        for k in steps:
-            onward[2 * k].wait_recv()
-            onward[2 * k + 1].wait_recv()
-            accumulate(it, [part(across, k), part(across, k + third)])
+        for copy in turned:
+            copy.wait_recv()
+        accumulate(now, [h for k in steps for h in (part(right, k), part(left, k + third))])
+        for some in (range(third - 1), range(third - 1, third)):
+            for k in some:
+                onward[2 * k].wait_recv()
+                onward[2 * k + 1].wait_recv()
+            accumulate(now, [h for k in some for h in (part(across, k), part(across, k + third))])
 
         for g in range(columns // 128):
             block = zacc[:, pl.ds(g * 128, 128)].reshape(4, 8, 128)
@@ -286,6 +315,8 @@
         start_space(lambda s: tiles_out.at[s], tiles_in, it, tile_send, tile_recv)
         tiles_in[it, me] = tiles_out[me]
 
+        if first:
+            turn(high, high_t)
         all_but_one(space_in, it, space_recv.at[it])
         factor_y[...] = inverse_factor(unpack(sum_of(space_in, it, ns)))
         all_but_one(space_in, it, space_send)
@@ -296,24 +327,34 @@
         sums[it, me] = sum_of(tiles_in, it, ns)
         start_space(lambda s: sums.at[it, me], sums, it, sum_send, sum_recv)
         all_but_one(tiles_in, it, tile_send)
+        if first:
+            turn(low, low_t)
         all_but_one(sums, it, sum_recv.at[it])
         gathered = sums[it].reshape(R, 8, 128)
         for g in range(columns // 128):
             block = gathered[g * 4 : g * 4 + 4].reshape(R, 128)
             zfull[:, g * 128 : g * 128 + 128] = exact(factor_y[...], block)
 
-        @pl.when(it < ITERS)
-        def _():
+        def framed():
             stacked = split(zfull[...])
             zst[...] = stacked
             gram_in[it + 1, mx] = pack(gram_of(stacked))
             for d in range(1, nx):
                 peer_copy(gram_in, it + 1, d, gram_send, gram_recv).start()
 
+        if first:
+            framed()
+        else:
+            pl.when(it < ITERS)(framed)
         all_but_one(sums, it, sum_send)
+
+    iteration(0, True)
+
+    def later(it, carry):
+        iteration(it, False)
         return carry
 
-    lax.fori_loop(0, ITERS + 1, iteration, 0)
+    lax.fori_loop(1, ITERS + 1, later, 0)
 
     slices = columns // MODES
     zfull[...] = zfull[...] * (1.0 / math.sqrt(total_rows))
@@ -345,7 +386,7 @@
         )
 
     for h in range(pieces):
-        ypart[h] = exact(factor_y[...], yfull[ITERS, h]) * math.sqrt(total_rows)
+        ypart[h] = exact(factor_y[...], yfull[ITERS % 2, h]) * math.sqrt(total_rows)
         write(h).start()
 
     for d in range(1, nx):
@@ -391,12 +432,14 @@
             scratch_shapes=[
                 pltpu.VMEM((pieces, prows, columns), BF16),
                 pltpu.VMEM((pieces, prows, columns), BF16),
-                pltpu.VMEM((4, prows, columns), F32),
+                pltpu.VMEM((2 * nx, columns, rows // (2 * nx)), BF16),
+                pltpu.VMEM((2 * nx, columns, rows // (2 * nx)), BF16),
+                pltpu.VMEM((2, prows, columns), F32),
                 pltpu.VMEM((2 * R, columns), BF16),
                 pltpu.VMEM((pieces, R, prows), F32),
-                pltpu.VMEM((steps, 2, PIECES // 2, R, prows), F32),
-                pltpu.VMEM((steps, 2, PIECES, R, prows), F32),
-                pltpu.VMEM((steps, pieces, R, prows), F32),
+                pltpu.VMEM((2, 2, PIECES // 2, R, prows), F32),
+                pltpu.VMEM((2, 2, PIECES, R, prows), F32),
+                pltpu.VMEM((2, pieces, R, prows), F32),
                 pltpu.VMEM((R, columns), F32),
                 pltpu.VMEM((R, columns), F32),
                 pltpu.VMEM((ns, per, 8, 128), F32),
@@ -408,8 +451,7 @@
                 pltpu.VMEM((R, MODES + 128), F32),
                 pltpu.VMEM((nx, R, MODES + 128), F32),
                 pltpu.VMEM((R, R), F32),
-                pltpu.VMEM((R, R), F32),
-                dma((4,)),
+                dma((2,)),
                 dma((36,)),
                 dma((steps, 36)),
                 dma,

time: 180 us -> 162 us (0.900)
  Pallas kernels: 174 us -> 156 us
    pallas_call x1, Pallas kernels: 174 us -> 156 us  [shards(): pl.pallas_call(functools.partial(kernel, ns, nx, rows * ns, slices * R *...]
where the time goes in v3:
time: 162 us
  Pallas kernels  156 us (96%)
  local copies, waits for them, and re-layouts  4.76 us (3%)
    pallas_call x1, Pallas kernels, shards(): pl.pallas_call(functools.partial(kernel, ns, nx, rows * ns, slices * R *...  156 us
    unnamed x3, local copies, waits for them, and re-layouts  4.76 us

profile of v3, /device:TPU:1, one launch (start us, length us, event | category | flops | bytes accessed | tf_op | source)
XLA Modules:
  0.0 161.7 jit_solution(13072163825799473988)
XLA Ops:
  0.6 156.3 %shard_map.58 = (f32[32,6144]{1,0:T(8,128)}, f32[32,128]{1,0:T(8,128)}, f32[32,256]{1,0:T(8,128)}) custom-call(f32[6144,1024]{1,0:T(8,128)} %snap.1, f32[32,1024]{1,0:T(8,128)} %bitcast.2, f32[32,256]{1,0:T(8,128)} %bitcast.3), custom_call_target="tpu_custom_call" | custom-call | tf_op jit(solution)/shard_map/pallas_call | solution.py:415
  157.0 2.1 %copy.9 = f32[32,6144]{1,0:T(8,128)} copy(f32[32,6144]{1,0:T(8,128)} %get-tuple-element.6) | data formatting | bytes 1572864
  159.0 1.3 copy.10
  160.3 1.4 copy.11

commit v4 on v3

--- a/solution.py
+++ b/solution.py
@@ -89,10 +89,12 @@
     sides = [0, 1] * third + [1, 0] * third + [0, 1] * third * 2
     places = [(quarters[n] * 2 + sides[n], n % 6 // 2) for n in range(4 * PIECES)]
 
-    def load(n):
+    grouped = [base + 2 * k + side for base in range(0, 4 * PIECES, PIECES) for side in (0, 1) for k in steps]
+
+    def load(i):
         return pltpu.make_async_copy(
-            snap.at[pl.ds(pl.multiple_of(order[n] * prows, prows), prows), :],
-            stage.at[n % loads], load_sem.at[n % loads],
+            snap.at[pl.ds(pl.multiple_of(order[grouped[i]] * prows, prows), prows), :],
+            stage.at[i % loads], load_sem.at[i % loads],
         )
 
     for n in range(loads):
@@ -109,22 +111,22 @@
         pl.semaphore_signal(barrier, inc=1, device_id=(me, lax.rem(mx + d, nx)), device_id_type=MESH)
 
     zst[...] = split(sketch[...])
-    pl.semaphore_wait(barrier, ns - 1 + nx - 1)
-
-    def fetch(n):
-        load(n).wait()
-
-        def cut(i, carry):
-            at = pl.ds(pl.multiple_of(i * 16, 16), 16)
-            value = stage[n % loads, at, :]
+
+    def fetch(i):
+        load(i).wait()
+        n = grouped[i]
+
+        def cut(row, carry):
+            at = pl.ds(pl.multiple_of(row * 16, 16), 16)
+            value = stage[i % loads, at, :]
             top = value.astype(BF16)
             high[order[n], at, :] = top
             low[order[n], at, :] = (value - top.astype(F32)).astype(BF16)
             return carry
 
         lax.fori_loop(0, prows // 16, cut, 0)
-        if n + loads < pieces:
-            load(n + loads).start()
+        if i + loads < pieces:
+            load(i + loads).start()
 
     def product(n, first):
         h = order[n]
@@ -149,10 +151,15 @@
         lax.fori_loop(0, pieces // third, one, 0)
 
     def in_turn(numbers, first, ready):
+        if first:
+            for at in range(numbers[0], numbers[-1] + 1, third):
+                for i in range(at, at + third):
+                    fetch(i)
+                for n, value in [(grouped[i], product(grouped[i], True)) for i in range(at, at + third)]:
+                    ready(n, value)
+            return
         ahead = None
         for n in numbers:
-            if first:
-                fetch(n)
             value = product(n, first)
             if ahead is not None:
                 ready(*ahead)
@@ -214,14 +221,16 @@
 
     def iteration(it, first):
         now = it % 2
-        far_copies, plain_copies, merged_copies = [], [], []
+        far_copies, plain_copies, merged_copies = {}, {}, []
 
         def send_far(n, value):
             k, side = divmod(n, 2)
+            if first and not far_copies:
+                pl.semaphore_wait(barrier, ns - 1 + nx - 1)
             ypart[order[n]] = value
             copy = along_x(ypart.at[order[n]], first_in.at[now, side, k], n, it, left if side else right)
             copy.start()
-            far_copies.append(copy)
+            far_copies[n] = copy
 
         def send_plain(n, value):
             k, side = divmod(n - len(far), 2)
@@ -229,16 +238,18 @@
             slot = second_in.at[now, side, k if side else k + third]
             copy = along_x(ypart.at[order[n]], slot, n, it, left if side else right)
             copy.start()
-            plain_copies.append(copy)
-
-        def send(n, value):
-            (send_far if n < len(far) else send_plain)(n, value)
+            plain_copies[n - len(far)] = copy
 
         def keep(n, value):
             ypart[order[n]] = value
 
         begun, base = len(far) + len(plain), pieces - len(own)
-        in_turn(range(begun), first, send)
+        in_turn(range(len(far)), first, send_far)
+        if not first:
+            gram_in[it, mx] = pack(gram_of(zst[...]))
+            for d in range(1, nx):
+                peer_copy(gram_in, it, d, gram_send, gram_recv).start()
+        in_turn(range(len(far), begun), first, send_plain)
         in_turn(range(begun, base), first, keep)
         for m, h in enumerate(merged):
             k, side = divmod(m, 2)
@@ -265,25 +276,34 @@
             spread.append(copy)
             return copy
 
-        for copy in merged_copies + plain_copies:
-            copy.wait_recv()
-        value = jnp.concatenate(
-            [
-                ypart[h] + second_in[now, 0, m // 2 + m % 2 * third] + second_in[now, 1, m // 2 + m % 2 * third]
-                for m, h in enumerate(own)
-            ],
-            axis=1,
-        )
-        if factor is not None:
-            value = exact(factor, value)
-        for m, h in enumerate(own):
-            yfull[now, h] = value[:, m * prows : (m + 1) * prows]
-        straight = [send_own(h, 18 + m, left if m % 2 else right) for m, h in enumerate(own)]
-        turned = [send_own(h, 24 + m, right if m % 2 else left) for m, h in enumerate(own)]
+        straight, turned, values = [], [], []
+
+        def cross(k):
+            for m in (2 * k, 2 * k + 1):
+                turned.append(send_own(own[m], 24 + m, right if m % 2 else left))
+
+        for k in steps:
+            value = []
+            for m in (2 * k, 2 * k + 1):
+                merged_copies[m].wait_recv()
+                plain_copies[m].wait_recv()
+            for m in (2 * k, 2 * k + 1):
+                piece = k + m % 2 * third
+                value.append(ypart[own[m]] + second_in[now, 0, piece] + second_in[now, 1, piece])
+            value = jnp.concatenate(value, axis=1)
+            if factor is not None:
+                value = exact(factor, value)
+            values.append(value)
+            for m in (2 * k, 2 * k + 1):
+                yfull[now, own[m]] = value[:, m % 2 * prows : (m % 2 + 1) * prows]
+                straight.append(send_own(own[m], 18 + m, left if m % 2 else right))
+            if k > 0:
+                cross(k - 1)
+        cross(third - 1)
 
         zacc[...] = jnp.zeros_like(zacc)
         accumulate(now, own)
-        own_in[it, mx] = pack(gram_of(split(value)))
+        own_in[it, mx] = pack(gram_of(split(jnp.concatenate(values, axis=1))))
         for d in range(1, nx):
             peer_copy(own_in, it, d, own_send, own_recv).start()
         onward = []
@@ -320,7 +340,7 @@
         all_but_one(space_in, it, space_recv.at[it])
         factor_y[...] = inverse_factor(unpack(sum_of(space_in, it, ns)))
         all_but_one(space_in, it, space_send)
-        for copy in far_copies + plain_copies + merged_copies + spread:
+        for copy in [*far_copies.values(), *plain_copies.values(), *merged_copies, *spread]:
             copy.wait_send()
 
         all_but_one(tiles_in, it, tile_recv.at[it])
@@ -335,17 +355,7 @@
             block = gathered[g * 4 : g * 4 + 4].reshape(R, 128)
             zfull[:, g * 128 : g * 128 + 128] = exact(factor_y[...], block)
 
-        def framed():
-            stacked = split(zfull[...])
-            zst[...] = stacked
-            gram_in[it + 1, mx] = pack(gram_of(stacked))
-            for d in range(1, nx):
-                peer_copy(gram_in, it + 1, d, gram_send, gram_recv).start()
-
-        if first:
-            framed()
-        else:
-            pl.when(it < ITERS)(framed)
+        zst[...] = split(zfull[...])
         all_but_one(sums, it, sum_send)
 
     iteration(0, True)
@@ -385,9 +395,13 @@
             ypart.at[h], basis_out.at[:, pl.ds(h * prows, prows)], out_sem.at[h]
         )
 
-    for h in range(pieces):
-        ypart[h] = exact(factor_y[...], yfull[ITERS % 2, h]) * math.sqrt(total_rows)
-        write(h).start()
+    for q in range(nx):
+        some = range(q * PIECES, (q + 1) * PIECES)
+        value = jnp.concatenate([yfull[ITERS % 2, h] for h in some], axis=1)
+        value = exact(factor_y[...], value) * math.sqrt(total_rows)
+        for h in some:
+            ypart[h] = value[:, h % PIECES * prows : (h % PIECES + 1) * prows]
+            write(h).start()
 
     for d in range(1, nx):
         last_copy(d).wait()
@@ -401,6 +415,15 @@
         write(h).wait()
 
 
+def move(basis, second, rest, basis_out, second_out, rest_out, sem):
+    pairs = ((basis, basis_out), (second, second_out), (rest, rest_out))
+    copies = [pltpu.make_async_copy(a, b, sem.at[n]) for n, (a, b) in enumerate(pairs)]
+    for copy in copies:
+        copy.start()
+    for copy in copies:
+        copy.wait()
+
+
 def solution(mesh):
     ns, nx = mesh.shape["space"], mesh.shape["param"]
 
@@ -412,7 +435,7 @@
         slices = columns // MODES
         steps = ITERS + 1
         dma = pltpu.SemaphoreType.DMA
-        return pl.pallas_call(
+        made = pl.pallas_call(
             functools.partial(kernel, ns, nx, rows * ns, slices * R * nx),
             out_shape=(
                 jax.ShapeDtypeStruct((R, rows), F32),
@@ -434,7 +457,7 @@
                 pltpu.VMEM((pieces, prows, columns), BF16),
                 pltpu.VMEM((2 * nx, columns, rows // (2 * nx)), BF16),
                 pltpu.VMEM((2 * nx, columns, rows // (2 * nx)), BF16),
-                pltpu.VMEM((2, prows, columns), F32),
+                pltpu.VMEM((4, prows, columns), F32),
                 pltpu.VMEM((2 * R, columns), BF16),
                 pltpu.VMEM((pieces, R, prows), F32),
                 pltpu.VMEM((2, 2, PIECES // 2, R, prows), F32),
@@ -451,7 +474,7 @@
                 pltpu.VMEM((R, MODES + 128), F32),
                 pltpu.VMEM((nx, R, MODES + 128), F32),
                 pltpu.VMEM((R, R), F32),
-                dma((2,)),
+                dma((4,)),
                 dma((36,)),
                 dma((steps, 36)),
                 dma,
@@ -472,6 +495,14 @@
                 collective_id=0, has_side_effects=True, vmem_limit_bytes=60 * 1024 * 1024
             ),
         )(snapshots, sketch.T, following.T)
+        anywhere = pl.BlockSpec(memory_space=pl.ANY)
+        return pl.pallas_call(
+            move,
+            out_shape=tuple(jax.ShapeDtypeStruct(one.shape, F32) for one in made),
+            in_specs=[anywhere] * 3,
+            out_specs=(anywhere,) * 3,
+            scratch_shapes=[dma((3,))],
+        )(*made)
 
     return jax.shard_map(
         shards,

time: 162 us -> 173 us (1.068)
  Pallas kernels: 156 us -> 172 us
  local copies, waits for them, and re-layouts: 4.76 us -> 0 us
    pallas_call x0 -> x1, Pallas kernels: none -> 26.4 us  [shards(): pl.pallas_call(move, out_shape=tuple((jax.ShapeDtypeStruct(one.shape, F32...]
    pallas_call x1, Pallas kernels: 156 us -> 146 us  [shards(): pl.pallas_call(functools.partial(kernel, ns, nx, rows * ns, slices * R *...]
    unnamed x3 -> x0, local copies, waits for them, and re-layouts: 4.76 us -> none
where the time goes in v4:
time: 173 us
  Pallas kernels  172 us (99%)
    pallas_call x1, Pallas kernels, shards(): pl.pallas_call(functools.partial(kernel, ns, nx, rows * ns, slices * R *...  146 us
    pallas_call x1, Pallas kernels, shards(): pl.pallas_call(move, out_shape=tuple((jax.ShapeDtypeStruct(one.shape, F32...  26.4 us

profile of v4, /device:TPU:1, one launch (start us, length us, event | category | flops | bytes accessed | tf_op | source)
XLA Modules:
  0.0 172.9 jit_solution(15095034490818105696)
XLA Ops:
  0.6 145.6 %shard_map.58 = (f32[32,6144]{1,0:T(8,128)}, f32[32,128]{1,0:T(8,128)}, f32[32,256]{1,0:T(8,128)}) custom-call(f32[6144,1024]{1,0:T(8,128)} %snap.1, f32[32,1024]{1,0:T(8,128)} %bitcast.2, f32[32,256]{1,0:T(8,128)} %bitcast.3), custom_call_target="tpu_custom_call" | custom-call | tf_op jit(solution)/shard_map/pallas_call | solution.py:438
  146.3 26.4 %shard_map.59 = (f32[32,6144]{1,0:T(8,128)}, f32[32,128]{1,0:T(8,128)}, f32[32,256]{1,0:T(8,128)}) custom-call(f32[32,6144]{1,0:T(8,128)} %get-tuple-element.6.basis, f32[32,128]{1,0:T(8,128)} %get-tuple-element.7.second, f32[32,256]{1,0:T(8,128)} %get-tuple-element.8.rest), custom_call_target="tpu_custom_call" | custom-call | tf_op jit(solution)/shard_map/pallas_call | solution.py:499

commit v5 on v4

--- a/solution.py
+++ b/solution.py
@@ -10,8 +10,10 @@
 
 MESH = pl.DeviceIdType.MESH
 R = 32
+MOVES = 4
 MODES = 256
 ITERS = 3
+BLOCK = 8
 PIECES = 6
 F32, BF16 = jnp.float32, jnp.bfloat16
 NN = (((1,), (0,)), ((), ()))
@@ -39,15 +41,28 @@
 
 
 def inverse_factor(gram):
+    wide = (R, 2 * R)
     rows = lax.broadcasted_iota(jnp.int32, (R, R), 0)
     columns = lax.broadcasted_iota(jnp.int32, (R, R), 1)
     eye = jnp.where(rows == columns, 1.0, 0.0).astype(F32)
     work = jnp.concatenate([gram, eye], axis=1)
-    below = lax.broadcasted_iota(jnp.int32, (R, 2 * R), 0)
-    for j in range(R - 1):
-        row = work[j : j + 1, :]
-        scaled = row / row[:, j : j + 1]
-        work = work - jnp.where(below > j, work[:, j : j + 1], 0.0) * scaled
+    below = lax.broadcasted_iota(jnp.int32, wide, 0)
+    for j in range(0, R, BLOCK):
+        row = [work[j + i : j + i + 1, :] for i in range(BLOCK)]
+        spread = [[jnp.broadcast_to(row[i][:, j + k : j + k + 1], (1, 2 * R)) for k in range(BLOCK)] for i in range(BLOCK)]
+        column = [jnp.broadcast_to(work[:, j + i : j + i + 1], wide) for i in range(BLOCK)]
+        for i in range(BLOCK):
+            if j + i == R - 1:
+                break
+            inverse = 1.0 / spread[i][i]
+            scaled = row[i] * inverse
+            work = work - jnp.where(below > j + i, column[i], 0.0) * scaled
+            for k in range(i + 1, BLOCK):
+                ratio = spread[i][k] * inverse
+                row[k] = row[k] - spread[i][k] * scaled
+                column[k] = column[k] - column[i] * ratio
+                for m in range(k, BLOCK):
+                    spread[k][m] = spread[k][m] - spread[i][m] * ratio
     diagonal = jnp.sum(jnp.where(rows == columns, work[:, :R], 0.0), axis=1, keepdims=True)
     return work[:, R:] / jnp.sqrt(diagonal)
 
@@ -89,12 +104,10 @@
     sides = [0, 1] * third + [1, 0] * third + [0, 1] * third * 2
     places = [(quarters[n] * 2 + sides[n], n % 6 // 2) for n in range(4 * PIECES)]
 
-    grouped = [base + 2 * k + side for base in range(0, 4 * PIECES, PIECES) for side in (0, 1) for k in steps]
-
-    def load(i):
+    def load(n):
         return pltpu.make_async_copy(
-            snap.at[pl.ds(pl.multiple_of(order[grouped[i]] * prows, prows), prows), :],
-            stage.at[i % loads], load_sem.at[i % loads],
+            snap.at[pl.ds(pl.multiple_of(order[n] * prows, prows), prows), :],
+            stage.at[n % loads], load_sem.at[n % loads],
         )
 
     for n in range(loads):
@@ -112,27 +125,19 @@
 
     zst[...] = split(sketch[...])
 
-    def fetch(i):
-        load(i).wait()
-        n = grouped[i]
-
-        def cut(row, carry):
-            at = pl.ds(pl.multiple_of(row * 16, 16), 16)
-            value = stage[i % loads, at, :]
-            top = value.astype(BF16)
-            high[order[n], at, :] = top
-            low[order[n], at, :] = (value - top.astype(F32)).astype(BF16)
-            return carry
-
-        lax.fori_loop(0, prows // 16, cut, 0)
-        if i + loads < pieces:
-            load(i + loads).start()
-
     def product(n, first):
         h = order[n]
         if first:
-            pair = lax.dot_general(zst[...], high[h], NT, preferred_element_type=F32)
-            pair += lax.dot_general(zst[...], low[h], NT, preferred_element_type=F32)
+            load(n).wait()
+            value = stage[n % loads]
+            top = value.astype(BF16)
+            rest = (value - top.astype(F32)).astype(BF16)
+            high[h] = top
+            low[h] = rest
+            pair = lax.dot_general(zst[...], top, NT, preferred_element_type=F32)
+            pair += lax.dot_general(zst[...], rest, NT, preferred_element_type=F32)
+            if n + loads < pieces:
+                load(n + loads).start()
         else:
             side, k = places[n]
             at = pl.ds(k * prows, prows)
@@ -151,13 +156,6 @@
         lax.fori_loop(0, pieces // third, one, 0)
 
     def in_turn(numbers, first, ready):
-        if first:
-            for at in range(numbers[0], numbers[-1] + 1, third):
-                for i in range(at, at + third):
-                    fetch(i)
-                for n, value in [(grouped[i], product(grouped[i], True)) for i in range(at, at + third)]:
-                    ready(n, value)
-            return
         ahead = None
         for n in numbers:
             value = product(n, first)
@@ -415,12 +413,19 @@
         write(h).wait()
 
 
-def move(basis, second, rest, basis_out, second_out, rest_out, sem):
-    pairs = ((basis, basis_out), (second, second_out), (rest, rest_out))
-    copies = [pltpu.make_async_copy(a, b, sem.at[n]) for n, (a, b) in enumerate(pairs)]
-    for copy in copies:
+def move(basis, second, rest, basis_out, second_out, rest_out, held, held_second, held_rest, sem, out_sem):
+    width = basis.shape[1] // MOVES
+    spans = [pl.ds(n * width, width) for n in range(MOVES)]
+    ways = [(basis.at[:, at], held.at[:, at], basis_out.at[:, at]) for at in spans]
+    ways += [(second, held_second, second_out), (rest, held_rest, rest_out)]
+    ins = [pltpu.make_async_copy(a, b, sem.at[n]) for n, (a, b, c) in enumerate(ways)]
+    outs = [pltpu.make_async_copy(b, c, out_sem.at[n]) for n, (a, b, c) in enumerate(ways)]
+    for copy in ins:
         copy.start()
-    for copy in copies:
+    for one, other in zip(ins, outs):
+        one.wait()
+        other.start()
+    for copy in outs:
         copy.wait()
 
 
@@ -501,7 +506,7 @@
             out_shape=tuple(jax.ShapeDtypeStruct(one.shape, F32) for one in made),
             in_specs=[anywhere] * 3,
             out_specs=(anywhere,) * 3,
-            scratch_shapes=[dma((3,))],
+            scratch_shapes=[pltpu.VMEM(one.shape, F32) for one in made] + [dma((MOVES + 2,)), dma((MOVES + 2,))],
         )(*made)
 
     return jax.shard_map(

time: 173 us -> 144 us (0.83)
  Pallas kernels: 172 us -> 143 us
    pallas_call x1, Pallas kernels: 26.4 us -> 2.01 us  [shards(): pl.pallas_call(move, out_shape=tuple((jax.ShapeDtypeStruct(one.shape, F32...]
    pallas_call x1, Pallas kernels: 146 us -> 141 us  [shards(): pl.pallas_call(functools.partial(kernel, ns, nx, rows * ns, slices * R *...]
where the time goes in v5:
time: 144 us
  Pallas kernels  143 us (99%)
    pallas_call x1, Pallas kernels, shards(): pl.pallas_call(functools.partial(kernel, ns, nx, rows * ns, slices * R *...  141 us

profile of v5, /device:TPU:1, one launch (start us, length us, event | category | flops | bytes accessed | tf_op | source)
XLA Modules:
  0.0 143.9 jit_solution(10895990507294262363)
XLA Ops:
  0.6 141.1 %shard_map.58 = (f32[32,6144]{1,0:T(8,128)}, f32[32,128]{1,0:T(8,128)}, f32[32,256]{1,0:T(8,128)}) custom-call(f32[6144,1024]{1,0:T(8,128)} %snap.1, f32[32,1024]{1,0:T(8,128)} %bitcast.2, f32[32,256]{1,0:T(8,128)} %bitcast.3), custom_call_target="tpu_custom_call" | custom-call | tf_op jit(solution)/shard_map/pallas_call | solution.py:443
  141.7 2.0 %shard_map.59 = (f32[32,6144]{1,0:T(8,128)}, f32[32,128]{1,0:T(8,128)}, f32[32,256]{1,0:T(8,128)}) custom-call(f32[32,6144]{1,0:T(8,128)} %get-tuple-element.6.basis, f32[32,128]{1,0:T(8,128)} %get-tuple-element.7.second, f32[32,256]{1,0:T(8,128)} %get-tuple-element.8.rest), custom_call_target="tpu_custom_call" | custom-call | tf_op jit(solution)/shard_map/pallas_call | solution.py:504

commit v6 on v5

--- a/solution.py
+++ b/solution.py
@@ -77,11 +77,11 @@
 
 def kernel(
     ns, nx, total_rows, unfold_rows,
-    snap, sketch, following, basis_out, second_out, rest_out,
-    high, low, high_t, low_t, stage, zst, ypart, first_in, second_in, yfull, zacc, zfull,
+    snap, sketch_in, following_in, basis_out, second_out, rest_out,
+    sketch, following, high, low, high_t, low_t, stage, zst, ypart, first_in, second_in, yfull, zacc, zfull,
     tiles_out, tiles_in, sums, gram_in, own_in, space_in, last_out, last_in,
     factor_y,
-    load_sem, send_sem, recv_sem, tile_send, tile_recv, sum_send, sum_recv,
+    small_sem, load_sem, send_sem, recv_sem, tile_send, tile_recv, sum_send, sum_recv,
     gram_send, gram_recv, own_send, own_recv, space_send, space_recv, last_send, last_recv, out_sem,
 ):
     me, mx = lax.axis_index("space"), lax.axis_index("param")
@@ -110,8 +110,14 @@
             stage.at[n % loads], load_sem.at[n % loads],
         )
 
+    small = [
+        pltpu.make_async_copy(sketch_in, sketch, small_sem.at[0]),
+        pltpu.make_async_copy(following_in, following, small_sem.at[1]),
+    ]
+    small[0].start()
     for n in range(loads):
         load(n).start()
+    small[1].start()
 
     barrier = pltpu.get_barrier_semaphore()
 
@@ -123,6 +129,7 @@
     for d in range(1, nx):
         pl.semaphore_signal(barrier, inc=1, device_id=(me, lax.rem(mx + d, nx)), device_id_type=MESH)
 
+    small[0].wait()
     zst[...] = split(sketch[...])
 
     def product(n, first):
@@ -223,9 +230,8 @@
 
         def send_far(n, value):
             k, side = divmod(n, 2)
-            if first and not far_copies:
-                pl.semaphore_wait(barrier, ns - 1 + nx - 1)
-            ypart[order[n]] = value
+            if not first:
+                ypart[order[n]] = value
             copy = along_x(ypart.at[order[n]], first_in.at[now, side, k], n, it, left if side else right)
             copy.start()
             far_copies[n] = copy
@@ -242,8 +248,13 @@
             ypart[order[n]] = value
 
         begun, base = len(far) + len(plain), pieces - len(own)
-        in_turn(range(len(far)), first, send_far)
-        if not first:
+        if first:
+            in_turn(range(len(far)), first, keep)
+            pl.semaphore_wait(barrier, ns - 1 + nx - 1)
+            for n in range(len(far)):
+                send_far(n, None)
+        else:
+            in_turn(range(len(far)), first, send_far)
             gram_in[it, mx] = pack(gram_of(zst[...]))
             for d in range(1, nx):
                 peer_copy(gram_in, it, d, gram_send, gram_recv).start()
@@ -295,15 +306,16 @@
             for m in (2 * k, 2 * k + 1):
                 yfull[now, own[m]] = value[:, m % 2 * prows : (m % 2 + 1) * prows]
                 straight.append(send_own(own[m], 18 + m, left if m % 2 else right))
-            if k > 0:
+            if 0 < k < third - 1:
                 cross(k - 1)
-        cross(third - 1)
-
-        zacc[...] = jnp.zeros_like(zacc)
-        accumulate(now, own)
         own_in[it, mx] = pack(gram_of(split(jnp.concatenate(values, axis=1))))
         for d in range(1, nx):
             peer_copy(own_in, it, d, own_send, own_recv).start()
+        cross(third - 2)
+
+        cross(third - 1)
+        zacc[...] = jnp.zeros_like(zacc)
+        accumulate(now, own)
         onward = []
         for k in steps:
             straight[2 * k].wait_recv()
@@ -348,12 +360,13 @@
         if first:
             turn(low, low_t)
         all_but_one(sums, it, sum_recv.at[it])
-        gathered = sums[it].reshape(R, 8, 128)
+        gathered, blocks = sums[it].reshape(R, 8, 128), []
         for g in range(columns // 128):
             block = gathered[g * 4 : g * 4 + 4].reshape(R, 128)
-            zfull[:, g * 128 : g * 128 + 128] = exact(factor_y[...], block)
-
-        zst[...] = split(zfull[...])
+            blocks.append(block)
+        whole = exact(factor_y[...], jnp.concatenate(blocks, axis=1))
+        zst[...] = split(whole)
+        zfull[...] = whole
         all_but_one(sums, it, sum_send)
 
     iteration(0, True)
@@ -364,6 +377,7 @@
 
     lax.fori_loop(1, ITERS + 1, later, 0)
 
+    small[1].wait()
     slices = columns // MODES
     zfull[...] = zfull[...] * (1.0 / math.sqrt(total_rows))
     sketched, rest = [], jnp.zeros((R, MODES), F32)
@@ -447,17 +461,15 @@
                 jax.ShapeDtypeStruct((R, slices * R), F32),
                 jax.ShapeDtypeStruct((R, MODES), F32),
             ),
-            in_specs=[
-                pl.BlockSpec(memory_space=pl.ANY),
-                pl.BlockSpec(memory_space=pltpu.VMEM),
-                pl.BlockSpec(memory_space=pltpu.VMEM),
-            ],
+            in_specs=[pl.BlockSpec(memory_space=pl.ANY)] * 3,
             out_specs=(
                 pl.BlockSpec(memory_space=pl.ANY),
                 pl.BlockSpec(memory_space=pltpu.VMEM),
                 pl.BlockSpec(memory_space=pltpu.VMEM),
             ),
             scratch_shapes=[
+                pltpu.VMEM((R, columns), F32),
+                pltpu.VMEM((R, MODES), F32),
                 pltpu.VMEM((pieces, prows, columns), BF16),
                 pltpu.VMEM((pieces, prows, columns), BF16),
                 pltpu.VMEM((2 * nx, columns, rows // (2 * nx)), BF16),
@@ -479,6 +491,7 @@
                 pltpu.VMEM((R, MODES + 128), F32),
                 pltpu.VMEM((nx, R, MODES + 128), F32),
                 pltpu.VMEM((R, R), F32),
+                dma((2,)),
                 dma((4,)),
                 dma((36,)),
                 dma((steps, 36)),

time: 144 us -> 142 us (0.986)
  Pallas kernels: 143 us -> 141 us
    pallas_call x1, Pallas kernels: 141 us -> 139 us  [shards(): pl.pallas_call(functools.partial(kernel, ns, nx, rows * ns, slices * R *...]
where the time goes in v6:
time: 142 us
  Pallas kernels  141 us (99%)
    pallas_call x1, Pallas kernels, shards(): pl.pallas_call(functools.partial(kernel, ns, nx, rows * ns, slices * R *...  139 us

profile of v6, /device:TPU:1, one launch (start us, length us, event | category | flops | bytes accessed | tf_op | source)
XLA Modules:
  0.0 142.3 jit_solution(12246924130972132680)
XLA Ops:
  0.6 139.5 %shard_map.58 = (f32[32,6144]{1,0:T(8,128)}, f32[32,128]{1,0:T(8,128)}, f32[32,256]{1,0:T(8,128)}) custom-call(f32[6144,1024]{1,0:T(8,128)} %snap.1, f32[32,1024]{1,0:T(8,128)} %bitcast.2, f32[32,256]{1,0:T(8,128)} %bitcast.3), custom_call_target="tpu_custom_call" | custom-call | tf_op jit(solution)/shard_map/pallas_call | solution.py:457
  140.1 2.0 %shard_map.59 = (f32[32,6144]{1,0:T(8,128)}, f32[32,128]{1,0:T(8,128)}, f32[32,256]{1,0:T(8,128)}) custom-call(f32[32,6144]{1,0:T(8,128)} %get-tuple-element.6.basis, f32[32,128]{1,0:T(8,128)} %get-tuple-element.7.second, f32[32,256]{1,0:T(8,128)} %get-tuple-element.8.rest), custom_call_target="tpu_custom_call" | custom-call | tf_op jit(solution)/shard_map/pallas_call | solution.py:517

commit v7 on v6

--- a/solution.py
+++ b/solution.py
@@ -254,10 +254,11 @@
             for n in range(len(far)):
                 send_far(n, None)
         else:
-            in_turn(range(len(far)), first, send_far)
+            in_turn(range(2), first, send_far)
             gram_in[it, mx] = pack(gram_of(zst[...]))
             for d in range(1, nx):
                 peer_copy(gram_in, it, d, gram_send, gram_recv).start()
+            in_turn(range(2, len(far)), first, send_far)
         in_turn(range(len(far), begun), first, send_plain)
         in_turn(range(begun, base), first, keep)
         for m, h in enumerate(merged):
@@ -306,14 +307,11 @@
             for m in (2 * k, 2 * k + 1):
                 yfull[now, own[m]] = value[:, m % 2 * prows : (m % 2 + 1) * prows]
                 straight.append(send_own(own[m], 18 + m, left if m % 2 else right))
-            if 0 < k < third - 1:
-                cross(k - 1)
         own_in[it, mx] = pack(gram_of(split(jnp.concatenate(values, axis=1))))
         for d in range(1, nx):
             peer_copy(own_in, it, d, own_send, own_recv).start()
-        cross(third - 2)
-
-        cross(third - 1)
+        for k in steps:
+            cross(k)
         zacc[...] = jnp.zeros_like(zacc)
         accumulate(now, own)
         onward = []
@@ -329,14 +327,14 @@
         space_in[it, me] = sum_of(own_in, it, nx)
         start_space(lambda s: space_in.at[it, me], space_in, it, space_send, space_recv)
 
-        for copy in turned:
-            copy.wait_recv()
-        accumulate(now, [h for k in steps for h in (part(right, k), part(left, k + third))])
-        for some in (range(third - 1), range(third - 1, third)):
-            for k in some:
-                onward[2 * k].wait_recv()
-                onward[2 * k + 1].wait_recv()
-            accumulate(now, [h for k in some for h in (part(across, k), part(across, k + third))])
+        for k in steps:
+            turned[2 * k].wait_recv()
+            turned[2 * k + 1].wait_recv()
+            accumulate(now, [part(right, k), part(left, k + third)])
+        for k in steps:
+            onward[2 * k].wait_recv()
+            onward[2 * k + 1].wait_recv()
+            accumulate(now, [part(across, k), part(across, k + third)])
 
         for g in range(columns // 128):
             block = zacc[:, pl.ds(g * 128, 128)].reshape(4, 8, 128)

time: 142 us -> 140 us (0.986)
  Pallas kernels: 141 us -> 139 us
    pallas_call x1, Pallas kernels: 139 us -> 137 us  [shards(): pl.pallas_call(functools.partial(kernel, ns, nx, rows * ns, slices * R *...]
where the time goes in v7:
time: 140 us
  Pallas kernels  139 us (99%)
    pallas_call x1, Pallas kernels, shards(): pl.pallas_call(functools.partial(kernel, ns, nx, rows * ns, slices * R *...  137 us

profile of v7, /device:TPU:1, one launch (start us, length us, event | category | flops | bytes accessed | tf_op | source)
XLA Modules:
  0.0 140.2 jit_solution(3385178754122042560)
XLA Ops:
  0.6 137.4 %shard_map.58 = (f32[32,6144]{1,0:T(8,128)}, f32[32,128]{1,0:T(8,128)}, f32[32,256]{1,0:T(8,128)}) custom-call(f32[6144,1024]{1,0:T(8,128)} %snap.1, f32[32,1024]{1,0:T(8,128)} %bitcast.2, f32[32,256]{1,0:T(8,128)} %bitcast.3), custom_call_target="tpu_custom_call" | custom-call | tf_op jit(solution)/shard_map/pallas_call | solution.py:455
  138.0 2.0 %shard_map.59 = (f32[32,6144]{1,0:T(8,128)}, f32[32,128]{1,0:T(8,128)}, f32[32,256]{1,0:T(8,128)}) custom-call(f32[32,6144]{1,0:T(8,128)} %get-tuple-element.6.basis, f32[32,128]{1,0:T(8,128)} %get-tuple-element.7.second, f32[32,256]{1,0:T(8,128)} %get-tuple-element.8.rest), custom_call_target="tpu_custom_call" | custom-call | tf_op jit(solution)/shard_map/pallas_call | solution.py:515

commit v8 on v7

--- a/solution.py
+++ b/solution.py
@@ -320,7 +320,7 @@
             onward.append(send_own(part(left, k), 30 + 2 * k, right))
             straight[2 * k + 1].wait_recv()
             onward.append(send_own(part(right, k + third), 31 + 2 * k, left))
-        accumulate(now, [h for k in steps for h in (part(left, k), part(right, k + third))])
+            accumulate(now, [part(left, k), part(right, k + third)])
 
         for d in range(1, nx):
             peer_copy(own_in, it, d, own_send, own_recv).wait()

time: 140 us -> 140 us (level)
  no operation moved by 1% of the time
where the time goes in v8:
time: 140 us
  Pallas kernels  139 us (99%)
    pallas_call x1, Pallas kernels, shards(): pl.pallas_call(functools.partial(kernel, ns, nx, rows * ns, slices * R *...  137 us

profile of v8, /device:TPU:1, one launch (start us, length us, event | category | flops | bytes accessed | tf_op | source)
XLA Modules:
  0.0 140.2 jit_solution(4861249154514355966)
XLA Ops:
  0.6 137.4 %shard_map.58 = (f32[32,6144]{1,0:T(8,128)}, f32[32,128]{1,0:T(8,128)}, f32[32,256]{1,0:T(8,128)}) custom-call(f32[6144,1024]{1,0:T(8,128)} %snap.1, f32[32,1024]{1,0:T(8,128)} %bitcast.2, f32[32,256]{1,0:T(8,128)} %bitcast.3), custom_call_target="tpu_custom_call" | custom-call | tf_op jit(solution)/shard_map/pallas_call | solution.py:455
  138.0 2.0 %shard_map.59 = (f32[32,6144]{1,0:T(8,128)}, f32[32,128]{1,0:T(8,128)}, f32[32,256]{1,0:T(8,128)}) custom-call(f32[32,6144]{1,0:T(8,128)} %get-tuple-element.6.basis, f32[32,128]{1,0:T(8,128)} %get-tuple-element.7.second, f32[32,256]{1,0:T(8,128)} %get-tuple-element.8.rest), custom_call_target="tpu_custom_call" | custom-call | tf_op jit(solution)/shard_map/pallas_call | solution.py:515

commit v9 on v7

--- a/solution.py
+++ b/solution.py
@@ -177,7 +177,7 @@
             device_id=(me, x), device_id_type=MESH,
         )
 
-    def accumulate(it, some):
+    def accumulate(it, some, last=False):
         stacked = [split(yfull[it, h]) for h in some]
         for b in range(columns // 256):
             at = pl.ds(b * 256, 256)
@@ -186,7 +186,14 @@
                 one = lax.dot_general(a, high[h, :, at], NN, preferred_element_type=F32)
                 one += lax.dot_general(a, low[h, :, at], NN, preferred_element_type=F32)
                 pair = one if pair is None else pair + one
-            zacc[:, at] += fold(pair)
+            if not last:
+                zacc[:, at] += fold(pair)
+                continue
+            total = zacc[:, at] + fold(pair)
+            for g in (2 * b, 2 * b + 1):
+                block = total[:, g % 2 * 128 : g % 2 * 128 + 128].reshape(4, 8, 128)
+                for t in range(4):
+                    tiles_out[(g * 4 + t) // per, (g * 4 + t) % per] = block[t]
         return stacked
 
     def peer_copy(ref, it, d, send, recv):
@@ -334,12 +341,8 @@
         for k in steps:
             onward[2 * k].wait_recv()
             onward[2 * k + 1].wait_recv()
-            accumulate(now, [part(across, k), part(across, k + third)])
-
-        for g in range(columns // 128):
-            block = zacc[:, pl.ds(g * 128, 128)].reshape(4, 8, 128)
-            for t in range(4):
-                tiles_out[(g * 4 + t) // per, (g * 4 + t) % per] = block[t]
+            accumulate(now, [part(across, k), part(across, k + third)], k == third - 1)
+
         start_space(lambda s: tiles_out.at[s], tiles_in, it, tile_send, tile_recv)
         tiles_in[it, me] = tiles_out[me]
 

time: 140 us -> 141 us (level)
  no operation moved by 1% of the time
where the time goes in v9:
time: 141 us
  Pallas kernels  140 us (99%)
    pallas_call x1, Pallas kernels, shards(): pl.pallas_call(functools.partial(kernel, ns, nx, rows * ns, slices * R *...  138 us

profile of v9, /device:TPU:1, one launch (start us, length us, event | category | flops | bytes accessed | tf_op | source)
XLA Modules:
  0.0 140.5 jit_solution(6314146927333769226)
XLA Ops:
  0.6 137.7 %shard_map.58 = (f32[32,6144]{1,0:T(8,128)}, f32[32,128]{1,0:T(8,128)}, f32[32,256]{1,0:T(8,128)}) custom-call(f32[6144,1024]{1,0:T(8,128)} %snap.1, f32[32,1024]{1,0:T(8,128)} %bitcast.2, f32[32,256]{1,0:T(8,128)} %bitcast.3), custom_call_target="tpu_custom_call" | custom-call | tf_op jit(solution)/shard_map/pallas_call | solution.py:458
  138.3 2.0 %shard_map.59 = (f32[32,6144]{1,0:T(8,128)}, f32[32,128]{1,0:T(8,128)}, f32[32,256]{1,0:T(8,128)}) custom-call(f32[32,6144]{1,0:T(8,128)} %get-tuple-element.6.basis, f32[32,128]{1,0:T(8,128)} %get-tuple-element.7.second, f32[32,256]{1,0:T(8,128)} %get-tuple-element.8.rest), custom_call_target="tpu_custom_call" | custom-call | tf_op jit(solution)/shard_map/pallas_call | solution.py:518
